TPU v7x, 32 devices: a whole 2x2x4 slice. The times are simulated.
32 devices in a mesh: group: 2 (over y), expert: 4 (over z), segment: 2 (over core), attn: 2 (over x).
Axes of the slice: x: 2, y: 2, z: 4, core: 2. Of those that a mesh axis runs over, the one named last changes fastest.
Arguments:
- res_cache: bfloat16 [128, 256, 576], P(('group', 'expert', 'segment', 'attn')), parts along dimension 0, may hold values from -8 to 8
- res_scales: bfloat16 [128, 4, 256], P(('group', 'expert', 'segment', 'attn')), parts along dimension 0, may hold values from 0.125 to 1
- res_lengths: int32 [128], P(('group', 'expert', 'segment', 'attn')), parts along dimension 0, may hold values from 2 to 256, as said below
- res_query: bfloat16 [128, 128, 576], P(('group', 'expert', 'segment', 'attn')), parts along dimension 0, may hold values from -256 to 256
- new_cache: bfloat16 [512, 128, 576], P(('group', 'expert', 'segment', 'attn')), parts along dimension 0, may hold values from -8 to 8
- new_scales: bfloat16 [512, 4, 128], P(('group', 'expert', 'segment', 'attn')), parts along dimension 0, may hold values from 0.125 to 1
- new_lengths: int32 [512], P(('group', 'expert', 'segment', 'attn')), parts along dimension 0, may hold values from 2 to 128, as said below
- new_query: bfloat16 [512, 128, 576], P(('group', 'expert', 'segment', 'attn')), parts along dimension 0, may hold values from -256 to 256
- owner: int32 [512], P(('group', 'expert', 'segment', 'attn')), parts along dimension 0, may hold values from 0 to 3, as said below
Outputs:
- res_context: bfloat16 [128, 128, 512], P(('group', 'expert', 'segment', 'attn')), parts along dimension 0
- new_context: bfloat16 [512, 128, 512], P(('group', 'expert', 'segment', 'attn')), parts along dimension 0
- owned_cache: bfloat16 [1024, 128, 576], P(('group', 'expert', 'segment', 'attn')), parts along dimension 0
- owned_scales: bfloat16 [1024, 4, 128], P(('group', 'expert', 'segment', 'attn')), parts along dimension 0
There are 2 independent parts, one for each index of `group`. A program takes and returns all parts, laid end to end along the dimension named above; each array names one. Nothing has to cross between parts.
Inputs may be any that keep to these rules, and one draw needn't show every extreme that they name: `res_lengths`: every device holds a resident request of length 256. `new_lengths`: every device holds a new request of length 128. Of the 16 requests of one device at most 8 name the same owner; in every draw one owner index is named by exactly 8 requests of every device.
All inputs are finite; a program needn't handle non-finite values.
Results may differ from a plain program's by a relative error of at most 0.0039.
Values may be sent and summed in bfloat16 or wider, within the bound.
No kernel may reach another device: no remote copies, remote signals or barrier semaphores. Data moves between devices by JAX's collectives and lax.ppermute only.
A program may use at most 64 MiB of HBM per device.

v0:
```python
import functools
import jax
import jax.numpy as jnp
from jax import lax
from jax.experimental import pallas as pl
from jax.experimental.pallas import tpu as pltpu
from jax.sharding import PartitionSpec as P

LATENT = 512
BLOCK = 128
UNIT_BITS = 6
UNIT = 1 << UNIT_BITS
FIRST = 2
PLANS = ((12, 7), (13, 8), (14, 10), (16, 16))
FACT_BITS = 8
FACT = 1 << FACT_BITS

softmax_scale = 192.0 ** (-0.5)
MIB = 1 << 20
VMEM_LIMIT = 56 * MIB


def attend_kernel(lengths_ref, query_ref, cache_ref, scales_ref, *refs):
    out_ref = refs[-1]
    per_step, _, positions = cache_ref.shape
    blocks = LATENT // BLOCK
    contract_rows = (((0,), (0,)), ((), ()))
    contract_positions = (((1,), (1,)), ((), ()))
    for r in range(per_step):
        length = lengths_ref[pl.program_id(0) * per_step + r]
        factors = scales_ref[r].astype(jnp.float32)
        scores = lax.dot_general(
            query_ref[r, LATENT:, :], cache_ref[r, LATENT:, :], contract_rows, preferred_element_type=jnp.float32
        )
        for b in range(blocks):
            part = lax.dot_general(
                query_ref[r, b * BLOCK : (b + 1) * BLOCK, :],
                cache_ref[r, b * BLOCK : (b + 1) * BLOCK, :],
                contract_rows,
                preferred_element_type=jnp.float32,
            )
            scores = scores + part * factors[b : b + 1, :]
        live = lax.broadcasted_iota(jnp.int32, (1, positions), 1) < length
        scores = jnp.where(live, scores * softmax_scale, -jnp.inf)
        exponent = jnp.exp(scores - jnp.max(scores, axis=-1, keepdims=True))
        probabilities = exponent * (1.0 / jnp.sum(exponent, axis=-1, keepdims=True))
        for b in range(blocks):
            weights = (probabilities * factors[b : b + 1, :]).astype(jnp.bfloat16)
            out_ref[r, :, b * BLOCK : (b + 1) * BLOCK] = lax.dot_general(
                weights,
                cache_ref[r, b * BLOCK : (b + 1) * BLOCK, :],
                contract_positions,
                preferred_element_type=jnp.float32,
            ).astype(jnp.bfloat16)


def attend(query, cache, scales, lengths, per_step, after=()):
    requests, columns, heads = query.shape
    positions = cache.shape[2]
    return pl.pallas_call(
        attend_kernel,
        grid=(requests // per_step,),
        in_specs=[
            pl.BlockSpec(memory_space=pltpu.SMEM),
            pl.BlockSpec((per_step, columns, heads), lambda i: (i, 0, 0)),
            pl.BlockSpec((per_step, columns, positions), lambda i: (i, 0, 0)),
            pl.BlockSpec((per_step, scales.shape[1], positions), lambda i: (i, 0, 0)),
        ]
        + [pl.BlockSpec(memory_space=pl.ANY)] * len(after),
        out_specs=pl.BlockSpec((per_step, heads, LATENT), lambda i: (i, 0, 0)),
        out_shape=jax.ShapeDtypeStruct((requests, heads, LATENT), jnp.bfloat16),
        compiler_params=pltpu.CompilerParams(vmem_limit_bytes=VMEM_LIMIT),
        cost_estimate=pl.CostEstimate(
            flops=4 * requests * heads * positions * columns,
            bytes_accessed=2 * requests * (heads * (columns + LATENT) + positions * columns),
            transcendentals=requests * heads * positions,
        ),
    )(lengths, query, cache, scales, *after)


def stream_gap(rows, positions, units):
    window = units * 2 * UNIT
    shape = (window, 2 * positions) if rows == "window" else (2 * positions, window)
    first, second = lax.broadcasted_iota(jnp.int32, shape, 0), lax.broadcasted_iota(jnp.int32, shape, 1)
    lane, own = (first, second) if rows == "window" else (second, first)
    within = lane % (2 * UNIT)
    place = lane // (2 * UNIT) * UNIT + within % UNIT
    meet = within // UNIT == own // positions
    side = (1, 2 * positions) if rows == "window" else (2 * positions, 1)
    position = lax.broadcasted_iota(jnp.int32, side, 1 if rows == "window" else 0) % positions
    return jnp.where(meet, place - own % positions, -512).astype(jnp.bfloat16), position


def moving(gap, position, shift, length):
    wanted = jnp.where(position < length, shift, 512).astype(jnp.bfloat16)
    return jnp.where(gap == wanted, jnp.ones((), jnp.bfloat16), jnp.zeros((), jnp.bfloat16))


def pack_kernel(owner_ref, lengths_ref, scales_ref, cache_ref, after_ref, *refs):
    experts = 4
    outs, (held, acc, slots, tails, ends, ranks, in_sem, out_sem) = refs[:5], refs[5:]
    requests, columns, positions = cache_ref.shape
    blocks = scales_ref.shape[1]
    half = columns // 2
    units = outs[4].shape[1] // half + FIRST
    window = positions // UNIT + 1
    me = lax.axis_index("expert")
    parts = in_sem.shape[0]
    share = requests // parts

    def rows_of(unit):
        return pl.ds(pl.multiple_of(unit * half, half), half)

    def fetch(part):
        here = pl.ds(part * share, share)
        return pltpu.make_async_copy(cache_ref.at[here], held.at[here], in_sem.at[part])

    for part in range(parts):
        fetch(part).start()
    gap, position = stream_gap("request", positions, window)
    for k in range(experts):
        ends[k] = 0
        ranks[k] = 0
        acc[k, :half] = jnp.zeros((half, 2 * UNIT), jnp.bfloat16)
    slots[...] = jnp.zeros(slots.shape, jnp.float32)
    live = lax.broadcasted_iota(jnp.int32, (blocks, positions), 1)

    def place(i, _):
        k = (owner_ref[i] - me) & (experts - 1)
        length = lengths_ref[i]
        start, rank = ends[k], ranks[k]
        ends[k] = start + length
        ranks[k] = rank + 1
        slots[k, pl.ds(rank * blocks, blocks), :] = jnp.where(live < length, scales_ref[i].astype(jnp.float32), 0.0)
        unit, shift = start >> UNIT_BITS, start & (UNIT - 1)
        move = moving(gap, position, shift, length)
        both = jnp.concatenate([held[i, :half, :], held[i, half:, :]], axis=1)
        moved = jnp.dot(both, move, preferred_element_type=jnp.float32).astype(jnp.bfloat16)
        acc[k, rows_of(unit), :] += moved[:, : 2 * UNIT]
        for j in range(1, window):
            acc[k, rows_of(unit + j), :] = moved[:, 2 * UNIT * j : 2 * UNIT * (j + 1)]
        return 0

    for part in range(parts):
        fetch(part).wait()
        lax.fori_loop(part * share, (part + 1) * share, place, 0, unroll=2)
    tails[...] = slots[...].astype(jnp.bfloat16)
    copies = []

    def copy(source, target):
        copies.append(pltpu.make_async_copy(source, target, out_sem.at[len(copies)]))

    for k in range(experts):
        size = FIRST if k else units
        copy(acc.at[k, pl.ds(0, size * half)], outs[k].at[pl.ds(0, size * half)])
        copy(tails.at[k], outs[k].at[pl.ds(size * half, tails.shape[1])])
        if k:
            copy(acc.at[k, pl.ds(FIRST * half, (units - FIRST) * half)], outs[4].at[k - 1])
    for each in copies:
        each.start()
    for each in copies:
        each.wait()


def pack(owner, lengths, scales, cache, after, units, capacity):
    requests, columns, positions = cache.shape
    half = columns // 2
    window = positions // UNIT + 1
    tail = capacity * scales.shape[1]
    smem = pl.BlockSpec(memory_space=pltpu.SMEM)
    vmem = pl.BlockSpec(memory_space=pltpu.VMEM)
    hbm = pl.BlockSpec(memory_space=pl.ANY)
    lanes = 2 * UNIT
    shapes = [(units * half + tail, lanes)] + [(FIRST * half + tail, lanes)] * 3 + [(3, (units - FIRST) * half, lanes)]
    return pl.pallas_call(
        pack_kernel,
        in_specs=[smem, smem, vmem, hbm, hbm],
        out_specs=[hbm] * 5,
        out_shape=[jax.ShapeDtypeStruct(shape, jnp.bfloat16) for shape in shapes],
        scratch_shapes=[
            pltpu.VMEM(cache.shape, jnp.bfloat16),
            pltpu.VMEM((4, (units + window - 1) * half, lanes), jnp.bfloat16),
            pltpu.VMEM((4, tail, positions), jnp.float32),
            pltpu.VMEM((4, tail, positions), jnp.bfloat16),
            pltpu.SMEM((4,), jnp.int32),
            pltpu.SMEM((4,), jnp.int32),
            pltpu.SemaphoreType.DMA((4,)),
            pltpu.SemaphoreType.DMA((11,)),
        ],
        compiler_params=pltpu.CompilerParams(vmem_limit_bytes=VMEM_LIMIT),
        cost_estimate=pl.CostEstimate(flops=2 * requests * half * 256 * 384, bytes_accessed=8 * MIB, transcendentals=0),
    )(owner, lengths, scales, cache, after)


def unpack_kernel(facts_ref, chosen_ref, own, f1, f2, f3, rest, out_ref, scales_ref, *scratch):
    held, stage, tails, slots, starts, counts, sems, out_sem = scratch
    experts = 4
    requests = facts_ref.shape[1]
    capacity = out_ref.shape[0] // experts
    columns, positions = out_ref.shape[1], out_ref.shape[2]
    blocks = scales_ref.shape[1]
    half = columns // 2
    units = rest.shape[1] // half + FIRST
    window = positions // UNIT + 1
    me = lax.axis_index("expert")

    def rows_of(unit):
        return pl.ds(pl.multiple_of(unit * half, half), half)

    def source_of(k):
        return (me - k) & (experts - 1)

    def scan(k, _):
        def note(i, carry):
            rank, end = carry
            mine = facts_ref[k, i] >> FACT_BITS == me
            length = facts_ref[k, i] & (FACT - 1)

            @pl.when(mine)
            def _():
                starts[k, rank] = end
                counts[k, rank] = length

            return (jnp.where(mine, rank + 1, rank), jnp.where(mine, end + length, end))

        rank, end = lax.fori_loop(0, requests, note, (0, 0))
        starts[k, capacity] = rank
        counts[k, capacity] = (end + UNIT - 1) >> UNIT_BITS
        return 0

    lax.fori_loop(0, experts, scan, 0)
    for k, stream in enumerate((own, f1, f2, f3)):
        used = counts[k, capacity]
        size = FIRST if k else units

        def fetch(u, _):
            pltpu.make_async_copy(stream.at[rows_of(u)], held.at[k, rows_of(u)], sems.at[k]).start()
            return 0

        lax.fori_loop(0, jnp.minimum(used, size), fetch, 0)
        tail = pl.ds(size * half, capacity * blocks)
        pltpu.make_async_copy(stream.at[tail], tails.at[k], sems.at[experts]).start()
        if k:
            place = chosen_ref[1 + source_of(k)]

            def fetch_rest(u, _):
                pltpu.make_async_copy(
                    rest.at[place, rows_of(u - FIRST)], held.at[k, rows_of(u)], sems.at[k]
                ).start()
                return 0

            lax.fori_loop(FIRST, used, fetch_rest, 0)
    gap, position = stream_gap("window", positions, window)

    def write(k):
        there = out_ref.at[pl.ds(source_of(k) * capacity, capacity)]
        return pltpu.make_async_copy(stage.at[k], there, out_sem.at[k])

    def put_stream(k, _):
        used, ranks = counts[k, capacity], starts[k, capacity]

        def arrive(u, _):
            pltpu.make_async_copy(own.at[rows_of(0)], held.at[k, rows_of(0)], sems.at[k]).wait()
            return 0

        lax.fori_loop(0, used, arrive, 0)
        for j in range(window):
            held[k, rows_of(used + j), :] = jnp.zeros((half, 2 * UNIT), jnp.bfloat16)

        def put(pair, _):
            for rank in (2 * pair, 2 * pair + 1):
                filled = rank < ranks
                start, length = jnp.where(filled, starts[k, rank], 0), jnp.where(filled, counts[k, rank], 0)
                unit, shift = start >> UNIT_BITS, start & (UNIT - 1)
                move = moving(gap, position, shift, length)
                seen = jnp.concatenate([held[k, rows_of(unit + j), :] for j in range(window)], axis=1)
                moved = jnp.dot(seen, move, preferred_element_type=jnp.float32).astype(jnp.bfloat16)
                stage[k, rank, :half, :] = moved[:, :positions]
                stage[k, rank, half:, :] = moved[:, positions:]
            return 0

        def clear(pair, _):
            stage[k, pl.ds(2 * pair, 2)] = jnp.zeros((2, columns, positions), jnp.bfloat16)
            return 0

        pairs = (ranks + 1) >> 1
        lax.fori_loop(0, pairs, put, 0)
        lax.fori_loop(pairs, capacity // 2, clear, 0)
        write(k).start()
        return 0

    lax.fori_loop(0, experts, put_stream, 0)
    for k in range(experts):
        pltpu.make_async_copy(own.at[pl.ds(0, capacity * blocks)], tails.at[k], sems.at[experts]).wait()
    slots[...] = tails[...].astype(jnp.float32)
    for k in range(experts):
        for rank in range(capacity):
            scales_ref[source_of(k) * capacity + rank] = slots[k, rank * blocks : (rank + 1) * blocks, :].astype(
                jnp.bfloat16
            )
    for k in range(experts):
        write(k).wait()


def unpack(facts, chosen, own, firsts, rest, capacity, columns, positions, blocks):
    half = columns // 2
    units = rest.shape[1] // half + FIRST
    window = positions // UNIT + 1
    smem = pl.BlockSpec(memory_space=pltpu.SMEM)
    vmem = pl.BlockSpec(memory_space=pltpu.VMEM)
    hbm = pl.BlockSpec(memory_space=pl.ANY)
    return pl.pallas_call(
        unpack_kernel,
        in_specs=[smem, smem] + [hbm] * 5,
        out_specs=[hbm, vmem],
        out_shape=[
            jax.ShapeDtypeStruct((4 * capacity, columns, positions), jnp.bfloat16),
            jax.ShapeDtypeStruct((4 * capacity, blocks, positions), jnp.bfloat16),
        ],
        scratch_shapes=[
            pltpu.VMEM((4, (units + window) * half, 2 * UNIT), jnp.bfloat16),
            pltpu.VMEM((4, capacity, columns, positions), jnp.bfloat16),
            pltpu.VMEM((4, capacity * blocks, positions), jnp.bfloat16),
            pltpu.VMEM((4, capacity * blocks, positions), jnp.float32),
            pltpu.SMEM((4, capacity + 1), jnp.int32),
            pltpu.SMEM((4, capacity + 1), jnp.int32),
            pltpu.SemaphoreType.DMA((5,)),
            pltpu.SemaphoreType.DMA((4,)),
        ],
        compiler_params=pltpu.CompilerParams(vmem_limit_bytes=VMEM_LIMIT),
        cost_estimate=pl.CostEstimate(flops=2 * 32 * half * 256 * 384, bytes_accessed=10 * MIB, transcendentals=0),
    )(facts, chosen, own, *firsts, rest)


def routes(hot):
    if hot >= 2:
        return [[(3 - source, 3 - target) for source, target in pairs] for pairs in routes(3 - hot)]
    if hot == 0:
        return [
            [(1, 0), (0, 1), (2, 3), (3, 2)],
            [(2, 0), (1, 2)],
            [(3, 0), (1, 3)],
            [(2, 1), (0, 2)],
            [(3, 1), (0, 3)],
        ]
    return [
        [(0, 1), (1, 2), (2, 3)],
        [(2, 1), (1, 0), (3, 2)],
        [(3, 1), (1, 3)],
        [(2, 0), (0, 2)],
        [(3, 0), (0, 3)],
    ]


def places(hot, target):
    by = [any(owner == target for _, owner in pairs) for pairs in routes(hot)]
    kept = [place if by[place] else None for place in range(3)] + [None, None]
    free = [place for place in range(3) if not by[place]]
    for permute in (3, 4):
        if by[permute]:
            kept[permute] = free.pop(0)
    return kept


def choose_kernel(there_ref, here_ref, out_ref, loads_ref):
    experts = 4
    requests = here_ref.shape[1]
    me = lax.axis_index("expert")
    for k in range(experts):
        most = [jnp.int32(0)] * experts
        for ref in (there_ref, here_ref):

            def add(i, loads):
                owner, length = ref[k, i] >> FACT_BITS, ref[k, i] & (FACT - 1)
                return tuple(load + jnp.where(owner == o, length, 0) for o, load in enumerate(loads))

            loads = lax.fori_loop(0, requests, add, (jnp.int32(0),) * experts, unroll=4)
            most = [jnp.maximum(m, (load + UNIT - 1) >> UNIT_BITS) for m, load in zip(most, loads)]
        source = (me - k) & (experts - 1)
        for o in range(experts):
            loads_ref[source * experts + o] = most[o]
    load = [[loads_ref[source * experts + o] for o in range(experts)] for source in range(experts)]
    hot, highest = jnp.int32(0), jnp.int32(-1)
    for o in range(experts):
        worst = functools.reduce(jnp.maximum, [load[source][o] for source in range(experts) if source != o])
        hot = jnp.where(worst > highest, o, hot)
        highest = jnp.maximum(worst, highest)
    most, second = jnp.int32(0), jnp.int32(0)
    for h in range(experts):
        for permute, pairs in enumerate(routes(h)):
            for source, target in pairs:
                here = jnp.where(hot == h, load[source][target], 0)
                if permute < 3:
                    most = jnp.maximum(most, here)
                else:
                    second = jnp.maximum(second, here)
    plan = jnp.int32(len(PLANS) - 1)
    for p in range(len(PLANS) - 2, -1, -1):
        plan = jnp.where(jnp.logical_and(most <= PLANS[p][0], second <= PLANS[p][1]), p, plan)
    out_ref[0] = hot * len(PLANS) + plan
    for source in range(experts):
        kept = jnp.int32(0)
        for h in range(experts):
            for target in range(experts):
                for permute, pairs in enumerate(routes(h)):
                    if (source, target) in pairs:
                        here = jnp.logical_and(hot == h, me == target)
                        kept = jnp.where(here, places(h, target)[permute], kept)
        out_ref[1 + source] = kept


def choose(there, here):
    smem = pl.BlockSpec(memory_space=pltpu.SMEM)
    return pl.pallas_call(
        choose_kernel,
        in_specs=[smem, smem],
        out_specs=smem,
        out_shape=jax.ShapeDtypeStruct((5,), jnp.int32),
        scratch_shapes=[pltpu.SMEM((16,), jnp.int32)],
    )(there, here)


def crossed(pairs):
    return [(source * 2 + s, target * 2 + 1 - s) for source, target in pairs for s in range(2)]


def by_halves(branches, index, *operands):
    def run(low, high, *operands):
        if high - low == 1:
            return branches[low](*operands)
        middle = (low + high) // 2
        return lax.cond(
            index < middle, functools.partial(run, low, middle), functools.partial(run, middle, high), *operands
        )

    return run(0, len(branches), *operands)


def keep_kernel(hot, *refs):
    got, kept, held, arrived, left = refs[:5], *refs[5:]
    me = lax.axis_index("expert")
    for target in range(4):

        @pl.when(me == target)
        def _():
            steps = []
            for permute, place in enumerate(places(hot, target)):
                if place is not None:
                    size = pl.ds(0, got[permute].shape[0])
                    into = pltpu.make_async_copy(got[permute], held.at[place, size], arrived.at[place])
                    out = pltpu.make_async_copy(held.at[place, size], kept.at[place, size], left.at[place])
                    steps.append((into, out))
            for into, _ in steps:
                into.start()
            for into, out in steps:
                into.wait()
                out.start()
            for _, out in steps:
                out.wait()


def keep(hot, got, shape):
    hbm = pl.BlockSpec(memory_space=pl.ANY)
    return pl.pallas_call(
        functools.partial(keep_kernel, hot),
        in_specs=[hbm] * 5,
        out_specs=hbm,
        out_shape=jax.ShapeDtypeStruct(shape, jnp.bfloat16),
        scratch_shapes=[
            pltpu.VMEM(shape, jnp.bfloat16),
            pltpu.SemaphoreType.DMA((3,)),
            pltpu.SemaphoreType.DMA((3,)),
        ],
    )(*got)


def exchange_rest(streams, half, me, branch):
    axes = ("expert", "segment")

    def send(hot, plan):
        most, second = (size - FIRST for size in PLANS[plan])

        def run(streams, me):
            def stream_by(pairs, size):
                apart = jnp.int32(0)
                for source, target in pairs:
                    apart = jnp.where(me == source, (target - source) % 4 - 1, apart)
                return lax.dynamic_slice_in_dim(streams, apart, 1, 0)[0, : size * half]

            got = []
            for permute, pairs in enumerate(routes(hot)):
                size = most if permute < 3 else second
                got.append(lax.ppermute(stream_by(pairs, size), axes, crossed(pairs)))
            return keep(hot, got, streams.shape)

        return run

    branches = [send(hot, plan) for hot in range(4) for plan in range(len(PLANS))]
    return by_halves(branches, branch, streams, me)


def slot_layout(owner, experts, capacity):
    requests = owner.shape[0]
    indices = jnp.arange(requests, dtype=jnp.int32)
    earlier = indices[None, :] < indices[:, None]
    same_owner = owner[:, None] == owner[None, :]
    arrival_rank = jnp.sum(jnp.logical_and(same_owner, earlier), axis=1)
    target = owner * capacity + arrival_rank
    routing = target[None, :] == jnp.arange(experts * capacity, dtype=jnp.int32)[:, None]
    filled = jnp.any(routing, axis=1)
    source = jnp.sum(jnp.where(routing, indices[None, :], 0), axis=1)
    return (filled, source)


def pick_slots(values, filled, source):
    zero_value = jnp.zeros((), values.dtype)
    return jnp.where(filled[:, None, None], jnp.take(values, source, axis=0), zero_value)


def on_device(
    res_cache,
    res_scales,
    res_lengths,
    res_query,
    new_cache,
    new_scales,
    new_lengths,
    new_query,
    owner,
):
    experts = lax.axis_size("expert")
    sections = lax.axis_size("segment")
    requests, positions, columns = new_cache.shape
    capacity = max(2, 2 * requests // experts)
    swap = [(0, 1), (1, 0)]
    cache_t = jnp.transpose(new_cache, (0, 2, 1))

    def attention(*after):
        res_context = attend(
            jnp.transpose(res_query, (0, 2, 1)), jnp.transpose(res_cache, (0, 2, 1)), res_scales, res_lengths, 2
        )
        new_context = attend(jnp.transpose(new_query, (0, 2, 1)), cache_t, new_scales, new_lengths, 4, after)
        return res_context, new_context

    if experts != 4 or sections != 2 or positions % UNIT or columns % 32:
        live_rows = jnp.arange(positions)[None, :] < new_lengths[:, None]
        zero_value = jnp.zeros((), jnp.bfloat16)
        filled, source = slot_layout(owner, experts, capacity)
        send_cache = pick_slots(jnp.where(live_rows[:, :, None], new_cache, zero_value), filled, source)
        send_scales = pick_slots(jnp.where(live_rows[:, None, :], new_scales, zero_value), filled, source)
        got_cache = lax.all_to_all(send_cache, "expert", split_axis=0, concat_axis=0, tiled=True)
        got_scales = lax.all_to_all(send_scales, "expert", split_axis=0, concat_axis=0, tiled=True)
        owned_cache, owned_scales = lax.ppermute((got_cache, got_scales), "segment", swap)
        return (*attention(), owned_cache, owned_scales)

    me = lax.axis_index("expert")
    units = capacity * positions // UNIT
    axes = ("expert", "segment")

    def shifted(value, k):
        return lax.ppermute(value, axes, crossed([(e, (e + k) % 4) for e in range(4)]))

    facts = owner * FACT + new_lengths
    there = jnp.stack([shifted(facts, k) for k in range(4)])
    own, f1, f2, f3, streams = pack(owner, new_lengths, new_scales, cache_t, there, units, capacity)
    here = lax.ppermute(there, "segment", swap)
    firsts = [shifted(part, k) for k, part in ((1, f1), (2, f2), (3, f3))]
    own = lax.ppermute(own, "segment", swap)
    chosen = choose(there, here)
    res_context, new_context = attention(chosen)
    streams, chosen, own, firsts, res_context, new_context = lax.optimization_barrier(
        (streams, chosen, own, firsts, res_context, new_context)
    )
    rest = exchange_rest(streams, columns // 2, me, chosen[0])
    owned, owned_scales = unpack(there, chosen, own, firsts, rest, capacity, columns, positions, new_scales.shape[1])
    return (res_context, new_context, jnp.transpose(owned, (0, 2, 1)), owned_scales)


def solution(mesh):
    placed = (
        P(("group", "expert", "segment", "attn"), None, None),
        P(("group", "expert", "segment", "attn"), None, None),
        P(("group", "expert", "segment", "attn")),
        P(("group", "expert", "segment", "attn"), None, None),
        P(("group", "expert", "segment", "attn"), None, None),
        P(("group", "expert", "segment", "attn"), None, None),
        P(("group", "expert", "segment", "attn")),
        P(("group", "expert", "segment", "attn"), None, None),
        P(("group", "expert", "segment", "attn")),
    )
    return jax.shard_map(
        on_device,
        mesh=mesh,
        in_specs=placed,
        out_specs=(
            P(("group", "expert", "segment", "attn"), None, None),
            P(("group", "expert", "segment", "attn"), None, None),
            P(("group", "expert", "segment", "attn"), None, None),
            P(("group", "expert", "segment", "attn"), None, None),
        ),
        check_vma=False,
    )
```

profile of v0, /device:TPU:8, one launch (start us, length us, event | category | flops | bytes accessed | tf_op | source)
XLA Modules:
  0.0 108.8 jit_solution(17528279575033034491)
XLA Ops:
  0.6 0.7 multiply_add_fusion
  1.3 2.8 %collective-permute-start.82 = (s32[16]{0:T(128)S(1)}, s32[16]{0:T(128)S(1)}, u32[]{:S(2)}, u32[]{:S(2)}) collective-permute-start(s32[16]{0:T(128)S(1)} %multiply_add_fusion), channel_id=1, source_target_pairs={{0,10},{2,8},{4,14},{6,12},{8,2},{10,0},{12,6},{14,4},{1,11},{3,9}... | collective-permute-start | bytes 200 | tf_op jit(solution)/shard_map/ppermute | solution.py:561
  4.1 1.9 %collective-permute-start.81 = (s32[16]{0:T(128)S(1)}, s32[16]{0:T(128)S(1)}, u32[]{:S(2)}, u32[]{:S(2)}) collective-permute-start(s32[16]{0:T(128)S(1)} %multiply_add_fusion), channel_id=1, source_target_pairs={{0,6},{2,4},{4,10},{6,8},{8,14},{10,12},{12,2},{14,0},{1,7},{3,5},... | collective-permute-start | bytes 200 | tf_op jit(solution)/shard_map/ppermute | solution.py:561
  8.1 6.1 %shard_map.120 = (bf16[4640,128]{1,0:T(8,128)(2,1)}, bf16[608,128]{1,0:T(8,128)(2,1)}, bf16[608,128]{1,0:T(8,128)(2,1)}, bf16[608,128]{1,0:T(8,128)(2,1)}, bf16[3,4032,128]{2,1,0:T(8,128)(2,1)S(1)}) custom-call(s32[16]{0:T(128)} %owner_ref.1, s32[16]{0:T(128)} %lengths_ref.5, bf16[16,4,128]{2,1,0:T(4,128)(2,1)} %scales_ref.5, ...), custom_call_target="tpu_custom_call" | custom-call | flops 905969664 | bytes 8388608 | tf_op jit(solution)/shard_map/pallas_call | solution.py:175
  14.6 1.8 %collective-permute-start.86 = (bf16[608,128]{1,0:T(8,128)(2,1)}, bf16[608,128]{1,0:T(8,128)(2,1)S(1)}, u32[]{:S(2)}, u32[]{:S(2)}) collective-permute-start(bf16[608,128]{1,0:T(8,128)(2,1)} %get-tuple-element.278), channel_id=1, source_target_pairs={{0,6},{2,4},{4,10},{6,8},{8,14},{10,12},{12,2},{14,0},{1,7},{3,5},... | collective-permute-start | bytes 466952 | tf_op jit(solution)/shard_map/ppermute | solution.py:561
  16.4 2.7 %collective-permute-start.87 = (bf16[608,128]{1,0:T(8,128)(2,1)}, bf16[608,128]{1,0:T(8,128)(2,1)S(1)}, u32[]{:S(2)}, u32[]{:S(2)}) collective-permute-start(bf16[608,128]{1,0:T(8,128)(2,1)} %get-tuple-element.279), channel_id=1, source_target_pairs={{0,10},{2,8},{4,14},{6,12},{8,2},{10,0},{12,6},{14,4},{1,11},{3,9}... | collective-permute-start | bytes 466952 | tf_op jit(solution)/shard_map/ppermute | solution.py:561
  19.1 4.1 %shard_map.122 = bf16[4,128,512]{2,1,0:T(8,128)(2,1)} custom-call(s32[4]{0:T(128)} %lengths_ref.4, bf16[4,576,128]{2,1,0:T(8,128)(2,1)} %bitcast.175, bf16[4,576,256]{2,1,0:T(8,128)(2,1)} %bitcast.174, bf16[4,4,256]{2,1,0:T(4,128)(2,1)} %scales_ref.4), custom_call_target="tpu_custom_call" | custom-call | flops 301989888 | bytes 2293760 | tf_op jit(solution)/shard_map/pallas_call | solution.py:60
  23.3 1.1 %collective-permute-done.84.here_ref = s32[4,16]{1,0:T(4,128)S(1)} collective-permute-done((s32[4,16]{1,0:T(4,128)S(1)}, s32[4,16]{1,0:T(4,128)S(1)}, u32[]{:S(2)}, u32[]{:S(2)}) %collective-permute-start.84) | collective-permute-done | bytes 288 | tf_op jit(solution)/shard_map/ppermute | solution.py:566
  24.9 2.4 %shard_map.121.refs_0_.chosen_ref = s32[5]{0:T(128)S(1)} custom-call(s32[4,16]{1,0:T(4,128)} %pad_add_fusion.after_ref.there_ref.facts_ref, s32[4,16]{1,0:T(4,128)} %copy-done.41), custom_call_target="tpu_custom_call" | custom-call | tf_op jit(solution)/shard_map/pallas_call | solution.py:414
  27.3 9.3 %shard_map.123 = bf16[16,128,512]{2,1,0:T(8,128)(2,1)} custom-call(s32[16]{0:T(128)} %lengths_ref.5, bf16[16,576,128]{2,1,0:T(8,128)(2,1)} %bitcast.171, bf16[16,576,128]{2,1,0:T(8,128)(2,1)} %bitcast.173, bf16[16,4,128]{2,1,0:T(4,128)(2,1)} %scales_ref.5, s32[5]{0:T(128)S(1)} %shard_map.121.refs_0_.chosen_ref), custom_call_target="tpu_custom_call" | custom-call | flops 603979776 | bytes 6815744 | tf_op jit(solution)/shard_map/pallas_call | solution.py:60
  37.3 65.4 %conditional.15 = (bf16[3,4032,128]{2,1,0:T(8,128)(2,1)}) conditional(s32[]{:T(128)} %convert_element_type.45, (s32[]{:T(128)S(1)}, s32[]{:T(128)}, bf16[3,4032,128]{2,1,0:T(8,128)(2,1)S(1)}) %tuple.174, (s32[]{:T(128)S(1)}, bf16[3,4032,128]{2,1,0:T(8,128)(2,1)S(1)}, s32[]{:T(128)}) %tuple.175), branch_computations={%region_0.15_spmd, %region_15.30_spmd} | conditional | flops 21 | bytes 47481440 | solution.py:432
  37.4 65.4 %conditional.13 = (bf16[3,4032,128]{2,1,0:T(8,128)(2,1)}) conditional(s32[]{:T(128)} %convert_element_type.43, (s32[]{:T(128)S(1)}, bf16[3,4032,128]{2,1,0:T(8,128)(2,1)S(1)}, s32[]{:T(128)}) %param.29, (s32[]{:T(128)S(1)}, s32[]{:T(128)}, bf16[3,4032,128]{2,1,0:T(8,128)(2,1)S(1)}) %tuple.82), branch_computations={%region_16.22_spmd, %region_23.29_spmd} | conditional | flops 19 | bytes 47481400 | solution.py:432
  37.4 65.3 %conditional.12 = (bf16[3,4032,128]{2,1,0:T(8,128)(2,1)}) conditional(s32[]{:T(128)} %convert_element_type.42, (s32[]{:T(128)S(1)}, s32[]{:T(128)}, bf16[3,4032,128]{2,1,0:T(8,128)(2,1)S(1)}) %param.28, (s32[]{:T(128)S(1)}, s32[]{:T(128)}, bf16[3,4032,128]{2,1,0:T(8,128)(2,1)S(1)}) %param.28), branch_computations={%region_24.25_spmd, %region_27.28_spmd} | conditional | flops 17 | bytes 47481384 | solution.py:432
  37.5 65.3 %conditional.11 = (bf16[3,4032,128]{2,1,0:T(8,128)(2,1)}) conditional(s32[]{:T(128)} %convert_element_type.41, (s32[]{:T(128)}, bf16[3,4032,128]{2,1,0:T(8,128)(2,1)S(1)}) %tuple.80, (s32[]{:T(128)}, bf16[3,4032,128]{2,1,0:T(8,128)(2,1)S(1)}) %tuple.80), branch_computations={%region_28.26_spmd, %region_29.27_spmd} | conditional | flops 15 | bytes 23445968 | solution.py:432
  37.5 1.5 %dynamic-slice_bitcast_fusion.62 = (bf16[3168,128]{1,0:T(8,128)(2,1)}, bf16[3168,128]{1,0:T(8,128)(2,1)}, bf16[3168,128]{1,0:T(8,128)(2,1)}) fusion(bf16[3,4032,128]{2,1,0:T(8,128)(2,1)S(1)} %get-tuple-element.246, s32[]{:T(128)S(6)} %select_n.561, s32[]{:T(128)S(6)} %select_n.560, s32[]{:T(128)S(6)} %select_n.558), kind=kLoop, calls=%fused_computation.70 | loop fusion | bytes 4866060 | tf_op jit(solution)/shard_map/cond/branch_1_fun/cond/branch_1_fun/cond/branch_1_fun/cond/branch_0_fun/squeeze | solution.py:488
  39.0 3.2 %collective-permute-start.72 = (bf16[3168,128]{1,0:T(8,128)(2,1)}, bf16[3168,128]{1,0:T(8,128)(2,1)}, u32[]{:S(2)}, u32[]{:S(2)}) collective-permute-start(bf16[3168,128]{1,0:T(8,128)(2,1)} %get-tuple-element.363), channel_id=1, source_target_pairs={{12,2},{14,0},{4,14},{6,12},{13,3},{15,1},{5,15},{7,13},{28,18},{3... | collective-permute-start | bytes 2433032 | tf_op jit(solution)/shard_map/cond/branch_1_fun/cond/branch_1_fun/cond/branch_1_fun/cond/branch_0_fun/ppermute | solution.py:493
  42.2 3.0 %collective-permute-start.71 = (bf16[3168,128]{1,0:T(8,128)(2,1)}, bf16[3168,128]{1,0:T(8,128)(2,1)}, u32[]{:S(2)}, u32[]{:S(2)}) collective-permute-start(bf16[3168,128]{1,0:T(8,128)(2,1)} %get-tuple-element.364), channel_id=1, source_target_pairs={{8,2},{10,0},{4,10},{6,8},{9,3},{11,1},{5,11},{7,9},{24,18},{26,16... | collective-permute-start | bytes 2433032 | tf_op jit(solution)/shard_map/cond/branch_1_fun/cond/branch_1_fun/cond/branch_1_fun/cond/branch_0_fun/ppermute | solution.py:493
  45.4 1.3 %collective-permute-start.74 = (bf16[1728,128]{1,0:T(8,128)(2,1)S(1)}, bf16[1728,128]{1,0:T(8,128)(2,1)S(1)}, u32[]{:S(2)}, u32[]{:S(2)}) collective-permute-start(bf16[1728,128]{1,0:T(8,128)(2,1)S(1)} %get-tuple-element.361), channel_id=1, source_target_pairs={{12,6},{14,4},{0,14},{2,12},{13,7},{15,5},{1,15},{3,13},{28,22},{3... | collective-permute-start | bytes 1327112 | tf_op jit(solution)/shard_map/cond/branch_1_fun/cond/branch_1_fun/cond/branch_1_fun/cond/branch_0_fun/ppermute | solution.py:493
  46.7 1.3 %collective-permute-start.73 = (bf16[1728,128]{1,0:T(8,128)(2,1)S(1)}, bf16[1728,128]{1,0:T(8,128)(2,1)S(1)}, u32[]{:S(2)}, u32[]{:S(2)}) collective-permute-start(bf16[1728,128]{1,0:T(8,128)(2,1)S(1)} %get-tuple-element.362), channel_id=1, source_target_pairs={{8,6},{10,4},{0,10},{2,8},{9,7},{11,5},{1,11},{3,9},{24,22},{26,20... | collective-permute-start | bytes 1327112 | tf_op jit(solution)/shard_map/cond/branch_1_fun/cond/branch_1_fun/cond/branch_1_fun/cond/branch_0_fun/ppermute | solution.py:493
  48.0 42.1 %collective-permute-done.74.refs_4_ = bf16[1728,128]{1,0:T(8,128)(2,1)S(1)} collective-permute-done((bf16[1728,128]{1,0:T(8,128)(2,1)S(1)}, bf16[1728,128]{1,0:T(8,128)(2,1)S(1)}, u32[]{:S(2)}, u32[]{:S(2)}) %collective-permute-start.74) | collective-permute-done | bytes 442400 | tf_op jit(solution)/shard_map/cond/branch_1_fun/cond/branch_1_fun/cond/branch_1_fun/cond/branch_0_fun/ppermute | solution.py:493
  90.1 9.6 %collective-permute-done.73.refs_3_ = bf16[1728,128]{1,0:T(8,128)(2,1)S(1)} collective-permute-done((bf16[1728,128]{1,0:T(8,128)(2,1)S(1)}, bf16[1728,128]{1,0:T(8,128)(2,1)S(1)}, u32[]{:S(2)}, u32[]{:S(2)}) %collective-permute-start.73) | collective-permute-done | bytes 442400 | tf_op jit(solution)/shard_map/cond/branch_1_fun/cond/branch_1_fun/cond/branch_1_fun/cond/branch_0_fun/ppermute | solution.py:493
  99.7 0.7 copy-done.31
  100.4 2.4 %branch_0_fun.15 = bf16[3,4032,128]{2,1,0:T(8,128)(2,1)} custom-call(bf16[3168,128]{1,0:T(8,128)(2,1)} %collective-permute-done.70.refs_0_, bf16[3168,128]{1,0:T(8,128)(2,1)} %collective-permute-done.71.refs_1_, bf16[3168,128]{1,0:T(8,128)(2,1)} %collective-permute-done.72.refs_2_, bf16[1728,128]{1,0:T(8,128)(2,1)} %copy-done.31, bf16[1728,128]{1,0:T(8,128)(2,1)} %copy-done.27), custom_call_target="tpu_custom_call" | custom-call | tf_op jit(solution)/shard_map/cond/branch_1_fun/cond/branch_1_fun/cond/branch_1_fun/cond/branch_0_fun/pallas_call | solution.py:464
  102.8 5.9 %shard_map.124 = (bf16[32,576,128]{2,1,0:T(8,128)(2,1)}, bf16[32,4,128]{2,1,0:T(4,128)(2,1)}) custom-call(s32[4,16]{1,0:T(4,128)} %pad_add_fusion.after_ref.there_ref.facts_ref, s32[5]{0:T(128)S(1)} %shard_map.121.refs_0_.chosen_ref, bf16[4640,128]{1,0:T(8,128)(2,1)} %collective-permute-done.85.own, bf16[608,128]{1,0:T(8,128)(2,1)} %copy-done.42, ...), custom_call_target="tpu_custom_call" | custom-call | flops 1811939328 | bytes 10485760 | tf_op jit(solution)/shard_map/pallas_call | solution.py:312
  (30 shorter events, 3.8 us)
Async XLA Ops:
  1.3 5.4 %collective-permute-start.83 = (s32[16]{0:T(128)S(1)}, s32[16]{0:T(128)S(1)}, u32[]{:S(2)}, u32[]{:S(2)}) collective-permute-start(s32[16]{0:T(128)S(1)} %multiply_add_fusion), channel_id=1, source_target_pairs={{0,14},{2,12},{4,2},{6,0},{8,6},{10,4},{12,10},{14,8},{1,15},{3,13... | collective-permute-start | bytes 200 | tf_op jit(solution)/shard_map/ppermute | solution.py:561
  1.3 5.4 %collective-permute-start.82 = (s32[16]{0:T(128)S(1)}, s32[16]{0:T(128)S(1)}, u32[]{:S(2)}, u32[]{:S(2)}) collective-permute-start(s32[16]{0:T(128)S(1)} %multiply_add_fusion), channel_id=1, source_target_pairs={{0,10},{2,8},{4,14},{6,12},{8,2},{10,0},{12,6},{14,4},{1,11},{3,9}... | collective-permute-start | bytes 200 | tf_op jit(solution)/shard_map/ppermute | solution.py:561
  4.1 3.2 %collective-permute-start.81 = (s32[16]{0:T(128)S(1)}, s32[16]{0:T(128)S(1)}, u32[]{:S(2)}, u32[]{:S(2)}) collective-permute-start(s32[16]{0:T(128)S(1)} %multiply_add_fusion), channel_id=1, source_target_pairs={{0,6},{2,4},{4,10},{6,8},{8,14},{10,12},{12,2},{14,0},{1,7},{3,5},... | collective-permute-start | bytes 200 | tf_op jit(solution)/shard_map/ppermute | solution.py:561
  6.0 1.5 %collective-permute-start.80 = (s32[16]{0:T(128)S(1)}, s32[16]{0:T(128)S(1)}, u32[]{:S(2)}, u32[]{:S(2)}) collective-permute-start(s32[16]{0:T(128)S(1)} %multiply_add_fusion), channel_id=1, source_target_pairs={{0,2},{2,0},{4,6},{6,4},{8,10},{10,8},{12,14},{14,12},{1,3},{3,1},... | collective-permute-start | bytes 200 | tf_op jit(solution)/shard_map/ppermute | solution.py:561
  8.1 15.1 %copy-start.40 = (s32[4,16]{1,0:T(4,128)S(1)}, s32[4,16]{1,0:T(4,128)}, u32[]{:S(2)}) copy-start(s32[4,16]{1,0:T(4,128)} %pad_add_fusion.after_ref.there_ref.facts_ref) | copy-start | bytes 772
  14.2 22.4 %collective-permute-start.85 = (bf16[4640,128]{1,0:T(8,128)(2,1)}, bf16[4640,128]{1,0:T(8,128)(2,1)}, u32[]{:S(2)}, u32[]{:S(2)}) collective-permute-start(bf16[4640,128]{1,0:T(8,128)(2,1)} %get-tuple-element.277), channel_id=1, source_target_pairs={{0,2},{2,0},{1,3},{3,1},{4,6},{6,4},{5,7},{7,5},{8,10},{10,8},{9,1... | collective-permute-start | bytes 3563528 | tf_op jit(solution)/shard_map/ppermute | solution.py:568
  14.6 22.0 %collective-permute-start.86 = (bf16[608,128]{1,0:T(8,128)(2,1)}, bf16[608,128]{1,0:T(8,128)(2,1)S(1)}, u32[]{:S(2)}, u32[]{:S(2)}) collective-permute-start(bf16[608,128]{1,0:T(8,128)(2,1)} %get-tuple-element.278), channel_id=1, source_target_pairs={{0,6},{2,4},{4,10},{6,8},{8,14},{10,12},{12,2},{14,0},{1,7},{3,5},... | collective-permute-start | bytes 466952 | tf_op jit(solution)/shard_map/ppermute | solution.py:561
  16.4 20.2 %collective-permute-start.87 = (bf16[608,128]{1,0:T(8,128)(2,1)}, bf16[608,128]{1,0:T(8,128)(2,1)S(1)}, u32[]{:S(2)}, u32[]{:S(2)}) collective-permute-start(bf16[608,128]{1,0:T(8,128)(2,1)} %get-tuple-element.279), channel_id=1, source_target_pairs={{0,10},{2,8},{4,14},{6,12},{8,2},{10,0},{12,6},{14,4},{1,11},{3,9}... | collective-permute-start | bytes 466952 | tf_op jit(solution)/shard_map/ppermute | solution.py:561
  19.1 17.5 %collective-permute-start.88 = (bf16[608,128]{1,0:T(8,128)(2,1)}, bf16[608,128]{1,0:T(8,128)(2,1)}, u32[]{:S(2)}, u32[]{:S(2)}) collective-permute-start(bf16[608,128]{1,0:T(8,128)(2,1)} %get-tuple-element.280), channel_id=1, source_target_pairs={{0,14},{2,12},{4,2},{6,0},{8,6},{10,4},{12,10},{14,8},{1,15},{3,13... | collective-permute-start | bytes 466952 | tf_op jit(solution)/shard_map/ppermute | solution.py:561
  23.2 1.2 %collective-permute-start.84 = (s32[4,16]{1,0:T(4,128)S(1)}, s32[4,16]{1,0:T(4,128)S(1)}, u32[]{:S(2)}, u32[]{:S(2)}) collective-permute-start(s32[4,16]{1,0:T(4,128)S(1)} %copy-done.40), channel_id=1, source_target_pairs={{0,2},{2,0},{1,3},{3,1},{4,6},{6,4},{5,7},{7,5},{8,10},{10,8},{9,1... | collective-permute-start | bytes 776 | tf_op jit(solution)/shard_map/ppermute | solution.py:566
  24.3 0.6 copy-start.41
  36.6 0.7 copy-start.42
  36.6 0.7 copy-start.43
  39.0 60.6 %collective-permute-start.72 = (bf16[3168,128]{1,0:T(8,128)(2,1)}, bf16[3168,128]{1,0:T(8,128)(2,1)}, u32[]{:S(2)}, u32[]{:S(2)}) collective-permute-start(bf16[3168,128]{1,0:T(8,128)(2,1)} %get-tuple-element.363), channel_id=1, source_target_pairs={{12,2},{14,0},{4,14},{6,12},{13,3},{15,1},{5,15},{7,13},{28,18},{3... | collective-permute-start | bytes 2433032 | tf_op jit(solution)/shard_map/cond/branch_1_fun/cond/branch_1_fun/cond/branch_1_fun/cond/branch_0_fun/ppermute | solution.py:493
  42.2 57.4 %collective-permute-start.71 = (bf16[3168,128]{1,0:T(8,128)(2,1)}, bf16[3168,128]{1,0:T(8,128)(2,1)}, u32[]{:S(2)}, u32[]{:S(2)}) collective-permute-start(bf16[3168,128]{1,0:T(8,128)(2,1)} %get-tuple-element.364), channel_id=1, source_target_pairs={{8,2},{10,0},{4,10},{6,8},{9,3},{11,1},{5,11},{7,9},{24,18},{26,16... | collective-permute-start | bytes 2433032 | tf_op jit(solution)/shard_map/cond/branch_1_fun/cond/branch_1_fun/cond/branch_1_fun/cond/branch_0_fun/ppermute | solution.py:493
  45.3 54.3 %collective-permute-start.70 = (bf16[3168,128]{1,0:T(8,128)(2,1)}, bf16[3168,128]{1,0:T(8,128)(2,1)}, u32[]{:S(2)}, u32[]{:S(2)}) collective-permute-start(bf16[3168,128]{1,0:T(8,128)(2,1)} %get-tuple-element.365), channel_id=1, source_target_pairs={{4,2},{6,0},{0,6},{2,4},{8,14},{10,12},{12,10},{14,8},{5,3},{7,1},... | collective-permute-start | bytes 2433032 | tf_op jit(solution)/shard_map/cond/branch_1_fun/cond/branch_1_fun/cond/branch_1_fun/cond/branch_0_fun/ppermute | solution.py:493
  45.4 44.7 %collective-permute-start.74 = (bf16[1728,128]{1,0:T(8,128)(2,1)S(1)}, bf16[1728,128]{1,0:T(8,128)(2,1)S(1)}, u32[]{:S(2)}, u32[]{:S(2)}) collective-permute-start(bf16[1728,128]{1,0:T(8,128)(2,1)S(1)} %get-tuple-element.361), channel_id=1, source_target_pairs={{12,6},{14,4},{0,14},{2,12},{13,7},{15,5},{1,15},{3,13},{28,22},{3... | collective-permute-start | bytes 1327112 | tf_op jit(solution)/shard_map/cond/branch_1_fun/cond/branch_1_fun/cond/branch_1_fun/cond/branch_0_fun/ppermute | solution.py:493
  46.7 53.0 %collective-permute-start.73 = (bf16[1728,128]{1,0:T(8,128)(2,1)S(1)}, bf16[1728,128]{1,0:T(8,128)(2,1)S(1)}, u32[]{:S(2)}, u32[]{:S(2)}) collective-permute-start(bf16[1728,128]{1,0:T(8,128)(2,1)S(1)} %get-tuple-element.362), channel_id=1, source_target_pairs={{8,6},{10,4},{0,10},{2,8},{9,7},{11,5},{1,11},{3,9},{24,22},{26,20... | collective-permute-start | bytes 1327112 | tf_op jit(solution)/shard_map/cond/branch_1_fun/cond/branch_1_fun/cond/branch_1_fun/cond/branch_0_fun/ppermute | solution.py:493
  90.1 9.6 %copy-start.27 = (bf16[1728,128]{1,0:T(8,128)(2,1)}, bf16[1728,128]{1,0:T(8,128)(2,1)S(1)}, u32[]{:S(2)}) copy-start(bf16[1728,128]{1,0:T(8,128)(2,1)S(1)} %collective-permute-done.74.refs_4_) | copy-start | bytes 1327108 | tf_op jit(solution)/shard_map/cond/branch_1_fun/cond/branch_1_fun/cond/branch_1_fun/cond
  99.6 0.8 copy-start.31
where the time goes:
time: 109 us
  waiting for transfers between devices  53.6 us (49%)
  Pallas kernels  30.1 us (28%)
  starting transfers between devices  19.2 us (18%)
  local copies, waits for them, and re-layouts  3.49 us (3%)
  other arithmetic  1.27 us (1%)
    ppermute x5, waiting for transfers between devices, run(): got.append(lax.ppermute(stream_by(pairs, size), axes, crossed(pairs)))  51.7 us
    pallas_call x2, Pallas kernels, attend(): pl.pallas_call(attend_kernel, grid=(requests // per_step,), in_specs=[pl....  13.4 us
    ppermute x7, starting transfers between devices, shifted(): lax.ppermute(value, axes, crossed([(e, (e + k) % 4) for e in range(4)]))  9.89 us
    ppermute x5, starting transfers between devices, run(): got.append(lax.ppermute(stream_by(pairs, size), axes, crossed(pairs)))  8.86 us
    pallas_call x1, Pallas kernels, pack(): pl.pallas_call(pack_kernel, in_specs=[smem, smem, vmem, hbm, hbm], out_sp...  6.13 us
    pallas_call x1, Pallas kernels, unpack(): pl.pallas_call(unpack_kernel, in_specs=[smem, smem] + [hbm] * 5, out_spec...  5.88 us
    pallas_call x1, Pallas kernels, keep(): pl.pallas_call(functools.partial(keep_kernel, hot), in_specs=[hbm] * 5, o...  2.39 us
    pallas_call x1, Pallas kernels, choose(): pl.pallas_call(choose_kernel, in_specs=[smem, smem], out_specs=smem, out_...  2.39 us
  transfers between devices with their start and end apart: 14, of which 5 were waited for; matrix products, arithmetic and copies ran while one was open for 0% of the time, Pallas kernels for 14%

commit v1 on v0

v1 whole, which is shorter than its diff:
```python
import functools
import jax
import jax.numpy as jnp
from jax import lax
from jax.experimental import pallas as pl
from jax.experimental.pallas import tpu as pltpu
from jax.sharding import PartitionSpec as P

LATENT = 512
BLOCK = 128
UNIT_BITS = 6
UNIT = 1 << UNIT_BITS
PLANS = ((12, 7), (13, 8), (14, 10), (16, 16))
FACT_BITS = 8
FACT = 1 << FACT_BITS

softmax_scale = 192.0 ** (-0.5)
MIB = 1 << 20
VMEM_LIMIT = 56 * MIB


def attend_kernel(lengths_ref, query_ref, cache_ref, scales_ref, out_ref):
    per_step, _, positions = cache_ref.shape
    blocks = LATENT // BLOCK
    contract_rows = (((0,), (0,)), ((), ()))
    contract_positions = (((1,), (1,)), ((), ()))
    for r in range(per_step):
        length = lengths_ref[pl.program_id(0) * per_step + r]
        factors = scales_ref[r].astype(jnp.float32)
        scores = lax.dot_general(
            query_ref[r, LATENT:, :], cache_ref[r, LATENT:, :], contract_rows, preferred_element_type=jnp.float32
        )
        for b in range(blocks):
            part = lax.dot_general(
                query_ref[r, b * BLOCK : (b + 1) * BLOCK, :],
                cache_ref[r, b * BLOCK : (b + 1) * BLOCK, :],
                contract_rows,
                preferred_element_type=jnp.float32,
            )
            scores = scores + part * factors[b : b + 1, :]
        live = lax.broadcasted_iota(jnp.int32, (1, positions), 1) < length
        scores = jnp.where(live, scores * softmax_scale, -jnp.inf)
        exponent = jnp.exp(scores - jnp.max(scores, axis=-1, keepdims=True))
        probabilities = exponent * (1.0 / jnp.sum(exponent, axis=-1, keepdims=True))
        for b in range(blocks):
            weights = (probabilities * factors[b : b + 1, :]).astype(jnp.bfloat16)
            out_ref[r, :, b * BLOCK : (b + 1) * BLOCK] = lax.dot_general(
                weights,
                cache_ref[r, b * BLOCK : (b + 1) * BLOCK, :],
                contract_positions,
                preferred_element_type=jnp.float32,
            ).astype(jnp.bfloat16)


def attend(query, cache, scales, lengths, per_step):
    requests, columns, heads = query.shape
    positions = cache.shape[2]
    return pl.pallas_call(
        attend_kernel,
        grid=(requests // per_step,),
        in_specs=[
            pl.BlockSpec(memory_space=pltpu.SMEM),
            pl.BlockSpec((per_step, columns, heads), lambda i: (i, 0, 0)),
            pl.BlockSpec((per_step, columns, positions), lambda i: (i, 0, 0)),
            pl.BlockSpec((per_step, scales.shape[1], positions), lambda i: (i, 0, 0)),
        ],
        out_specs=pl.BlockSpec((per_step, heads, LATENT), lambda i: (i, 0, 0)),
        out_shape=jax.ShapeDtypeStruct((requests, heads, LATENT), jnp.bfloat16),
        compiler_params=pltpu.CompilerParams(vmem_limit_bytes=VMEM_LIMIT),
        cost_estimate=pl.CostEstimate(
            flops=4 * requests * heads * positions * columns,
            bytes_accessed=2 * requests * (heads * (columns + LATENT) + positions * columns),
            transcendentals=requests * heads * positions,
        ),
    )(lengths, query, cache, scales)


def stream_gap(rows, positions, units):
    window = units * 2 * UNIT
    shape = (window, 2 * positions) if rows == "window" else (2 * positions, window)
    first, second = lax.broadcasted_iota(jnp.int32, shape, 0), lax.broadcasted_iota(jnp.int32, shape, 1)
    lane, own = (first, second) if rows == "window" else (second, first)
    within = lane % (2 * UNIT)
    place = lane // (2 * UNIT) * UNIT + within % UNIT
    meet = within // UNIT == own // positions
    side = (1, 2 * positions) if rows == "window" else (2 * positions, 1)
    position = lax.broadcasted_iota(jnp.int32, side, 1 if rows == "window" else 0) % positions
    return jnp.where(meet, place - own % positions, -512).astype(jnp.bfloat16), position


def moving(gap, position, shift, length):
    wanted = jnp.where(position < length, shift, 512).astype(jnp.bfloat16)
    return jnp.where(gap == wanted, jnp.ones((), jnp.bfloat16), jnp.zeros((), jnp.bfloat16))


def pack_kernel(owner_ref, lengths_ref, scales_ref, cache_ref, after_ref, out_ref, *scratch):
    held, acc, slots, ends, ranks, in_sem, out_sem = scratch
    experts = 4
    requests, columns, positions = cache_ref.shape
    blocks = scales_ref.shape[1]
    half = columns // 2
    tail = slots.shape[1]
    window = positions // UNIT + 1
    me = lax.axis_index("expert")
    parts = in_sem.shape[0]
    share = requests // parts

    def rows_of(unit):
        return pl.ds(pl.multiple_of(tail + unit * half, 16), half)

    def fetch(part):
        here = pl.ds(part * share, share)
        return pltpu.make_async_copy(cache_ref.at[here], held.at[here], in_sem.at[part])

    for part in range(parts):
        fetch(part).start()
    gap, position = stream_gap("request", positions, window)
    for k in range(experts):
        ends[k] = 0
        ranks[k] = 0
        acc[k, rows_of(0), :] = jnp.zeros((half, 2 * UNIT), jnp.bfloat16)
    slots[...] = jnp.zeros(slots.shape, jnp.float32)
    live = lax.broadcasted_iota(jnp.int32, (blocks, positions), 1)

    def place(i, _):
        k = (owner_ref[i] - me) & (experts - 1)
        length = lengths_ref[i]
        start, rank = ends[k], ranks[k]
        ends[k] = start + length
        ranks[k] = rank + 1
        slots[k, pl.ds(rank * blocks, blocks), :] = jnp.where(live < length, scales_ref[i].astype(jnp.float32), 0.0)
        unit, shift = start >> UNIT_BITS, start & (UNIT - 1)
        move = moving(gap, position, shift, length)
        both = jnp.concatenate([held[i, :half, :], held[i, half:, :]], axis=1)
        moved = jnp.dot(both, move, preferred_element_type=jnp.float32).astype(jnp.bfloat16)
        acc[k, rows_of(unit), :] += moved[:, : 2 * UNIT]
        for j in range(1, window):
            acc[k, rows_of(unit + j), :] = moved[:, 2 * UNIT * j : 2 * UNIT * (j + 1)]
        return 0

    for part in range(parts):
        fetch(part).wait()
        lax.fori_loop(part * share, (part + 1) * share, place, 0, unroll=2)
    acc[:, :tail, :] = slots[...].astype(jnp.bfloat16)
    rows = pl.ds(0, out_ref.shape[1])
    copies = [pltpu.make_async_copy(acc.at[k, rows], out_ref.at[k], out_sem.at[k]) for k in range(experts)]
    for each in copies:
        each.start()
    for each in copies:
        each.wait()


def pack(owner, lengths, scales, cache, after, units, capacity):
    requests, columns, positions = cache.shape
    half = columns // 2
    window = positions // UNIT + 1
    tail = capacity * scales.shape[1]
    smem = pl.BlockSpec(memory_space=pltpu.SMEM)
    vmem = pl.BlockSpec(memory_space=pltpu.VMEM)
    hbm = pl.BlockSpec(memory_space=pl.ANY)
    lanes = 2 * UNIT
    return pl.pallas_call(
        pack_kernel,
        in_specs=[smem, smem, vmem, hbm, hbm],
        out_specs=hbm,
        out_shape=jax.ShapeDtypeStruct((4, tail + units * half, lanes), jnp.bfloat16),
        scratch_shapes=[
            pltpu.VMEM(cache.shape, jnp.bfloat16),
            pltpu.VMEM((4, tail + (units + window - 1) * half, lanes), jnp.bfloat16),
            pltpu.VMEM((4, tail, positions), jnp.float32),
            pltpu.SMEM((4,), jnp.int32),
            pltpu.SMEM((4,), jnp.int32),
            pltpu.SemaphoreType.DMA((4,)),
            pltpu.SemaphoreType.DMA((4,)),
        ],
        compiler_params=pltpu.CompilerParams(vmem_limit_bytes=VMEM_LIMIT),
        cost_estimate=pl.CostEstimate(flops=2 * requests * half * 256 * 384, bytes_accessed=8 * MIB, transcendentals=0),
    )(owner, lengths, scales, cache, after)


def fours(hot):
    beside = hot ^ 1
    return (hot, beside, *(e for e in range(4) if e not in (hot, beside)))


def routes(hot):
    hot, beside, one, two = fours(hot)
    permutations = [[e ^ 1 for e in range(4)]]
    for a, b in ((hot, one), (hot, two), (beside, one), (beside, two)):
        permutations.append([b if e == a else a if e == b else e for e in range(4)])
    return permutations


def own_routes(hot):
    hot, beside, one, two = fours(hot)
    return {hot: (3, 4), beside: (1,), one: (2,), two: (1,)}


def pick(index, values):
    value = jnp.int32(values[0])
    for at in range(1, len(values)):
        value = jnp.where(index == at, values[at], value)
    return value


def unpack_kernel(hot, second, facts_ref, g0, g1, g2, g3, g4, out_ref, scales_ref, *scratch):
    held, stage, tails, slots, starts, counts, sems, out_sem = scratch
    got = (g0, g1, g2, g3, g4)
    experts = 4
    requests = facts_ref.shape[1]
    capacity = out_ref.shape[0] // experts
    columns, positions = out_ref.shape[1], out_ref.shape[2]
    blocks = scales_ref.shape[1]
    half = columns // 2
    tail = tails.shape[1]
    window = positions // UNIT + 1
    units = held.shape[1] // half - window
    me = lax.axis_index("expert")
    other = 1 - lax.axis_index("segment")

    def rows_of(unit):
        return pl.ds(pl.multiple_of(unit * half, 16), half)

    def units_of(unit):
        return pl.ds(pl.multiple_of(tail + unit * half, 16), half)

    def source_of(k):
        return (me - k) & (experts - 1)

    def scan(k, _):
        row = source_of(k) * 2 + other

        def note(i, carry):
            rank, end = carry
            mine = facts_ref[row, i] >> FACT_BITS == me
            length = facts_ref[row, i] & (FACT - 1)

            @pl.when(mine)
            def _():
                starts[k, rank] = end
                counts[k, rank] = length

            return (jnp.where(mine, rank + 1, rank), jnp.where(mine, end + length, end))

        rank, end = lax.fori_loop(0, requests, note, (0, 0))
        starts[k, capacity] = rank
        counts[k, capacity] = (end + UNIT - 1) >> UNIT_BITS
        return 0

    lax.fori_loop(0, experts, scan, 0)

    def fetch(ref, k, low, high, before):
        def one(u, _):
            pltpu.make_async_copy(ref.at[units_of(u - before)], held.at[k, rows_of(u)], sems.at[k]).start()
            return 0

        lax.fori_loop(low, high, one, 0)

    def fetch_stream(k, _):
        source = source_of(k)
        used = counts[k, capacity]
        routed = [pick(source, routes(hot)[permute]) == me for permute in range(5)]
        stays = [pick(me, [int(permute in own_routes(hot)[e]) for e in range(4)]) == 1 for permute in range(5)]
        for permute in range(5):
            held_units = (got[permute].shape[0] - tail) // half

            @pl.when(jnp.logical_and(routed[permute], jnp.logical_or(k > 0, stays[permute])))
            def _():
                if permute < 4:
                    pltpu.make_async_copy(got[permute].at[pl.ds(0, tail)], tails.at[k], sems.at[experts]).start()
                    fetch(got[permute], k, 0, jnp.minimum(used, held_units), 0)
                else:
                    split = jnp.logical_and(k == 0, me == hot)

                    @pl.when(jnp.logical_not(split))
                    def _():
                        pltpu.make_async_copy(got[permute].at[pl.ds(0, tail)], tails.at[k], sems.at[experts]).start()

                    before = jnp.where(split, min(second, units - second), 0)
                    fetch(got[permute], k, jnp.where(split, second, 0), used, before)

        return 0

    lax.fori_loop(0, experts, fetch_stream, 0)
    gap, position = stream_gap("window", positions, window)

    def write(k):
        there = out_ref.at[pl.ds(source_of(k) * capacity, capacity)]
        return pltpu.make_async_copy(stage.at[k], there, out_sem.at[k])

    def put_stream(k, _):
        used, ranks = counts[k, capacity], starts[k, capacity]

        def arrive(u, _):
            pltpu.make_async_copy(g0.at[units_of(0)], held.at[k, rows_of(0)], sems.at[k]).wait()
            return 0

        lax.fori_loop(0, used, arrive, 0)
        for j in range(window):
            held[k, rows_of(used + j), :] = jnp.zeros((half, 2 * UNIT), jnp.bfloat16)

        def put(pair, _):
            for rank in (2 * pair, 2 * pair + 1):
                filled = rank < ranks
                start, length = jnp.where(filled, starts[k, rank], 0), jnp.where(filled, counts[k, rank], 0)
                unit, shift = start >> UNIT_BITS, start & (UNIT - 1)
                move = moving(gap, position, shift, length)
                seen = jnp.concatenate([held[k, rows_of(unit + j), :] for j in range(window)], axis=1)
                moved = jnp.dot(seen, move, preferred_element_type=jnp.float32).astype(jnp.bfloat16)
                stage[k, rank, :half, :] = moved[:, :positions]
                stage[k, rank, half:, :] = moved[:, positions:]
            return 0

        def clear(pair, _):
            stage[k, pl.ds(2 * pair, 2)] = jnp.zeros((2, columns, positions), jnp.bfloat16)
            return 0

        pairs = (ranks + 1) >> 1
        lax.fori_loop(0, pairs, put, 0)
        lax.fori_loop(pairs, capacity // 2, clear, 0)
        write(k).start()
        return 0

    lax.fori_loop(0, experts, put_stream, 0)
    for k in range(experts):
        pltpu.make_async_copy(g0.at[pl.ds(0, tail)], tails.at[k], sems.at[experts]).wait()
    slots[...] = tails[...].astype(jnp.float32)

    def put_scales(k, _):
        for rank in range(capacity):
            scales_ref[source_of(k) * capacity + rank] = slots[k, rank * blocks : (rank + 1) * blocks, :].astype(
                jnp.bfloat16
            )
        return 0

    lax.fori_loop(0, experts, put_scales, 0)
    for k in range(experts):
        write(k).wait()


def unpack(hot, plan, facts, got, units, capacity, columns, positions, blocks):
    half = columns // 2
    window = positions // UNIT + 1
    smem = pl.BlockSpec(memory_space=pltpu.SMEM)
    vmem = pl.BlockSpec(memory_space=pltpu.VMEM)
    hbm = pl.BlockSpec(memory_space=pl.ANY)
    return pl.pallas_call(
        functools.partial(unpack_kernel, hot, PLANS[plan][1]),
        in_specs=[smem] + [hbm] * 5,
        out_specs=[hbm, vmem],
        out_shape=[
            jax.ShapeDtypeStruct((4 * capacity, columns, positions), jnp.bfloat16),
            jax.ShapeDtypeStruct((4 * capacity, blocks, positions), jnp.bfloat16),
        ],
        scratch_shapes=[
            pltpu.VMEM((4, (units + window) * half, 2 * UNIT), jnp.bfloat16),
            pltpu.VMEM((4, capacity, columns, positions), jnp.bfloat16),
            pltpu.VMEM((4, capacity * blocks, positions), jnp.bfloat16),
            pltpu.VMEM((4, capacity * blocks, positions), jnp.float32),
            pltpu.SMEM((4, capacity + 1), jnp.int32),
            pltpu.SMEM((4, capacity + 1), jnp.int32),
            pltpu.SemaphoreType.DMA((5,)),
            pltpu.SemaphoreType.DMA((4,)),
        ],
        compiler_params=pltpu.CompilerParams(vmem_limit_bytes=VMEM_LIMIT),
        cost_estimate=pl.CostEstimate(flops=2 * 32 * half * 256 * 384, bytes_accessed=10 * MIB, transcendentals=0),
    )(facts, *got)


def choose_kernel(facts_ref, out_ref):
    experts = 4
    rows, requests = facts_ref.shape
    load = [[jnp.int32(0)] * experts for _ in range(experts)]
    for row in range(rows):

        def add(i, sums):
            owner, length = facts_ref[row, i] >> FACT_BITS, facts_ref[row, i] & (FACT - 1)
            part = length << ((owner >> 1) << 4)
            odd = (owner & 1) == 1
            return (sums[0] + jnp.where(odd, 0, part), sums[1] + jnp.where(odd, part, 0))

        even, odd = lax.fori_loop(0, requests, add, (jnp.int32(0), jnp.int32(0)), unroll=8)
        for o, sums in enumerate((even, odd, even >> 16, odd >> 16)):
            units = ((sums & 0xFFFF) + UNIT - 1) >> UNIT_BITS
            load[row // 2][o] = jnp.maximum(load[row // 2][o], units)
    hot, highest = jnp.int32(0), jnp.int32(-1)
    for o in range(experts):
        worst = functools.reduce(jnp.maximum, [load[source][o] for source in range(experts) if source != o])
        hot = jnp.where(worst > highest, o, hot)
        highest = jnp.maximum(worst, highest)
    most, second = jnp.int32(0), jnp.int32(0)
    for h in range(experts):
        sizes = [jnp.int32(0), jnp.int32(0)]
        for permute, targets in enumerate(routes(h)):
            for source, target in enumerate(targets):
                if source != target:
                    sizes[permute // 3] = jnp.maximum(sizes[permute // 3], load[source][target])
        for e in range(experts):
            if e == h:
                sizes[1] = jnp.maximum(sizes[1], (load[e][e] + 1) >> 1)
            else:
                sizes[0] = jnp.maximum(sizes[0], load[e][e])
        most = jnp.where(hot == h, sizes[0], most)
        second = jnp.where(hot == h, sizes[1], second)
    plan = jnp.int32(len(PLANS) - 1)
    for p in range(len(PLANS) - 2, -1, -1):
        plan = jnp.where(jnp.logical_and(most <= PLANS[p][0], second <= PLANS[p][1]), p, plan)
    out_ref[0] = hot * len(PLANS) + plan


def choose(facts):
    smem = pl.BlockSpec(memory_space=pltpu.SMEM)
    return pl.pallas_call(
        choose_kernel,
        in_specs=[smem],
        out_specs=smem,
        out_shape=jax.ShapeDtypeStruct((1,), jnp.int32),
    )(facts)


def crossed(targets):
    return [(source * 2 + s, target * 2 + 1 - s) for source, target in enumerate(targets) for s in range(2)]


def by_halves(branches, index, operands):
    def run(low, high, operands):
        if high - low == 1:
            return branches[low](operands)
        middle = (low + high) // 2
        return lax.cond(
            index < middle, functools.partial(run, low, middle), functools.partial(run, middle, high), operands
        )

    return run(0, len(branches), operands)


def exchange(streams, facts, me, hot, plan, capacity, columns, positions, blocks):
    half = columns // 2
    tail = capacity * blocks
    units = (streams.shape[1] - tail) // half
    got = []
    for permute, targets in enumerate(routes(hot)):
        size = PLANS[plan][permute // 3]
        k = pick(me, [(target - source) % 4 for source, target in enumerate(targets)])
        first = jnp.int32(0)
        if permute == 4:
            first = jnp.where(me == hot, min(size, units - size) * half, 0)
        part = lax.dynamic_slice(streams, (k, first, jnp.int32(0)), (1, tail + size * half, streams.shape[2]))[0]
        got.append(lax.ppermute(part, ("expert", "segment"), crossed(targets)))
    return unpack(hot, plan, facts, got, units, capacity, columns, positions, blocks)


def slot_layout(owner, experts, capacity):
    requests = owner.shape[0]
    indices = jnp.arange(requests, dtype=jnp.int32)
    earlier = indices[None, :] < indices[:, None]
    same_owner = owner[:, None] == owner[None, :]
    arrival_rank = jnp.sum(jnp.logical_and(same_owner, earlier), axis=1)
    target = owner * capacity + arrival_rank
    routing = target[None, :] == jnp.arange(experts * capacity, dtype=jnp.int32)[:, None]
    filled = jnp.any(routing, axis=1)
    source = jnp.sum(jnp.where(routing, indices[None, :], 0), axis=1)
    return (filled, source)


def pick_slots(values, filled, source):
    zero_value = jnp.zeros((), values.dtype)
    return jnp.where(filled[:, None, None], jnp.take(values, source, axis=0), zero_value)


def on_device(
    res_cache,
    res_scales,
    res_lengths,
    res_query,
    new_cache,
    new_scales,
    new_lengths,
    new_query,
    owner,
):
    experts = lax.axis_size("expert")
    sections = lax.axis_size("segment")
    requests, positions, columns = new_cache.shape
    capacity = max(2, 2 * requests // experts)
    swap = [(0, 1), (1, 0)]
    cache_t = jnp.transpose(new_cache, (0, 2, 1))
    res_inputs = (jnp.transpose(res_query, (0, 2, 1)), jnp.transpose(res_cache, (0, 2, 1)), res_scales, res_lengths)
    inputs = (res_inputs, (jnp.transpose(new_query, (0, 2, 1)), cache_t, new_scales, new_lengths))

    def attention(res_inputs, new_inputs):
        return attend(*res_inputs, 1), attend(*new_inputs, 1)

    if experts != 4 or sections != 2 or positions % UNIT or columns % 32:
        live_rows = jnp.arange(positions)[None, :] < new_lengths[:, None]
        zero_value = jnp.zeros((), jnp.bfloat16)
        filled, source = slot_layout(owner, experts, capacity)
        send_cache = pick_slots(jnp.where(live_rows[:, :, None], new_cache, zero_value), filled, source)
        send_scales = pick_slots(jnp.where(live_rows[:, None, :], new_scales, zero_value), filled, source)
        got_cache = lax.all_to_all(send_cache, "expert", split_axis=0, concat_axis=0, tiled=True)
        got_scales = lax.all_to_all(send_scales, "expert", split_axis=0, concat_axis=0, tiled=True)
        owned_cache, owned_scales = lax.ppermute((got_cache, got_scales), "segment", swap)
        return (*attention(*inputs), owned_cache, owned_scales)

    me = lax.axis_index("expert")
    section = lax.axis_index("segment")
    units = capacity * positions // UNIT
    facts = owner * FACT + new_lengths
    sibling = lax.ppermute(facts, "segment", swap)
    chip = jnp.where(section == 0, jnp.stack([facts, sibling]), jnp.stack([sibling, facts]))
    chips = [chip] + [lax.ppermute(chip, "expert", [(e, (e + k) % 4) for e in range(4)]) for k in range(1, 4)]
    streams = pack(owner, new_lengths, new_scales, cache_t, sibling, units, capacity)
    facts = lax.dynamic_slice_in_dim(jnp.concatenate(chips[::-1] * 2), (3 - me) * 2, 8, 0)
    branch = choose(facts)[0]

    def take(hot, plan):
        def run(operands):
            streams, facts, *inputs = operands
            owned = exchange(streams, facts, me, hot, plan, capacity, columns, positions, new_scales.shape[1])
            return (*attention(*inputs), *owned)

        return run

    branches = [take(hot, plan) for hot in range(4) for plan in range(len(PLANS))]
    res_context, new_context, owned, owned_scales = by_halves(branches, branch, (streams, facts, *inputs))
    return (res_context, new_context, jnp.transpose(owned, (0, 2, 1)), owned_scales)


def solution(mesh):
    placed = (
        P(("group", "expert", "segment", "attn"), None, None),
        P(("group", "expert", "segment", "attn"), None, None),
        P(("group", "expert", "segment", "attn")),
        P(("group", "expert", "segment", "attn"), None, None),
        P(("group", "expert", "segment", "attn"), None, None),
        P(("group", "expert", "segment", "attn"), None, None),
        P(("group", "expert", "segment", "attn")),
        P(("group", "expert", "segment", "attn"), None, None),
        P(("group", "expert", "segment", "attn")),
    )
    return jax.shard_map(
        on_device,
        mesh=mesh,
        in_specs=placed,
        out_specs=(
            P(("group", "expert", "segment", "attn"), None, None),
            P(("group", "expert", "segment", "attn"), None, None),
            P(("group", "expert", "segment", "attn"), None, None),
            P(("group", "expert", "segment", "attn"), None, None),
        ),
        check_vma=False,
    )
```

time: 109 us -> 108 us (level)
  the two profiles are of different devices: /device:TPU:8 before, /device:TPU:0 now
where the time goes in v1:
time: 108 us
  waiting for transfers between devices  50 us (46%)
  Pallas kernels  31 us (29%)
  starting transfers between devices  10.9 us (10%)
  local copies, waits for them, and re-layouts  10.7 us (10%)
  loops' own time  2.7 us (2%)
  between operations  1.52 us (1%)
    ppermute x5, waiting for transfers between devices, exchange(): got.append(lax.ppermute(part, ('expert', 'segment'), crossed(targets)))  49.2 us
    pallas_call x2, Pallas kernels, attend(): pl.pallas_call(attend_kernel, grid=(requests // per_step,), in_specs=[pl....  15.6 us
    pallas_call x1, Pallas kernels, pack(): pl.pallas_call(pack_kernel, in_specs=[smem, smem, vmem, hbm, hbm], out_sp...  7.1 us
    ppermute x3, starting transfers between devices, on_device(): lax.ppermute(chip, 'expert', [(e, (e + k) % 4) for e in range(4)])  6.86 us
    pallas_call x1, Pallas kernels, unpack(): pl.pallas_call(functools.partial(unpack_kernel, hot, PLANS[plan][1]), in_...  6.29 us
    squeeze x2, local copies, waits for them, and re-layouts, exchange(): lax.dynamic_slice(streams, (k, first, jnp.int32(0)), (1, tail + size * ha...  4.9 us
    ppermute x5, starting transfers between devices, exchange(): got.append(lax.ppermute(part, ('expert', 'segment'), crossed(targets)))  3.58 us
    another operation x4, loops' own time, run(): lax.cond(index < middle, functools.partial(run, low, middle), functools.p...  2.7 us
  transfers between devices with their start and end apart: 9, of which 3 were waited for; matrix products, arithmetic and copies ran while one was open for 1% of the time, Pallas kernels for 21%

profile of v1, /device:TPU:0, one launch (start us, length us, event | category | flops | bytes accessed | tf_op | source)
XLA Modules:
  0.0 107.6 jit_solution(15301680182870338022)
XLA Ops:
  0.6 0.7 multiply_add_fusion
  1.8 0.8 collective-permute-done.80.after_ref
  2.6 2.9 %collective-permute-start.83 = (s32[2,16]{1,0:T(2,128)S(1)}, s32[2,16]{1,0:T(2,128)S(1)}, u32[]{:S(2)}, u32[]{:S(2)}) collective-permute-start(s32[2,16]{1,0:T(2,128)S(1)} %add_select_fusion), channel_id=1, source_target_pairs={{0,4},{4,8},{8,12},{12,0},{1,5},{5,9},{9,13},{13,1},{2,6},{6,10},{... | collective-permute-start | bytes 392 | tf_op jit(solution)/shard_map/ppermute | solution.py:511
  5.5 2.6 %collective-permute-start.82 = (s32[2,16]{1,0:T(2,128)S(1)}, s32[2,16]{1,0:T(2,128)S(1)}, u32[]{:S(2)}, u32[]{:S(2)}) collective-permute-start(s32[2,16]{1,0:T(2,128)S(1)} %add_select_fusion), channel_id=1, source_target_pairs={{0,8},{4,12},{8,0},{12,4},{1,9},{5,13},{9,1},{13,5},{2,10},{6,14},... | collective-permute-start | bytes 392 | tf_op jit(solution)/shard_map/ppermute | solution.py:511
  8.1 1.3 %collective-permute-start.81 = (s32[2,16]{1,0:T(2,128)S(1)}, s32[2,16]{1,0:T(2,128)}, u32[]{:S(2)}, u32[]{:S(2)}) collective-permute-start(s32[2,16]{1,0:T(2,128)S(1)} %add_select_fusion), channel_id=1, source_target_pairs={{0,12},{4,0},{8,4},{12,8},{1,13},{5,1},{9,5},{13,9},{2,14},{6,2},{... | collective-permute-start | bytes 392 | tf_op jit(solution)/shard_map/ppermute | solution.py:511
  9.5 7.1 %shard_map.125 = bf16[4,4640,128]{2,1,0:T(8,128)(2,1)} custom-call(s32[16]{0:T(128)} %owner_ref.1, s32[16]{0:T(128)} %lengths_ref.1, bf16[16,4,128]{2,1,0:T(4,128)(2,1)} %scales_ref.1, bf16[16,576,128]{2,1,0:T(8,128)(2,1)} %bitcast.168, s32[16]{0:T(128)} %copy-done.86), custom_call_target="tpu_custom_call" | custom-call | flops 905969664 | bytes 8388608 | tf_op jit(solution)/shard_map/pallas_call | solution.py:162
  16.6 0.5 copy-done.84
  17.2 0.6 copy-done.85
  17.7 2.6 %concatenate.3 = s32[16,16]{1,0:T(8,128)} concatenate(s32[2,16]{1,0:T(2,128)} %collective-permute-done.81, s32[2,16]{1,0:T(2,128)} %copy-done.85, s32[2,16]{1,0:T(2,128)} %copy-done.84, s32[2,16]{1,0:T(2,128)} %copy-done.83, s32[2,16]{1,0:T(2,128)} %collective-permute-done.81, s32[2,16]{1,0:T(2,128)} %copy-done.85, s32[2,16]{1,0:T(2,128)} %copy-done.84, s32[2,16]{1,0:T(2,128)} %copy-done.83), dimensions={0} | concatenate | bytes 2048 | tf_op jit(solution)/shard_map/concatenate | solution.py:513
  20.4 1.3 %constant_dynamic-slice_fusion.facts_ref = s32[8,16]{1,0:T(8,128)} fusion(s32[16,16]{1,0:T(8,128)} %concatenate.3, s32[]{:T(128)S(6)} %select_n.871), kind=kLoop, calls=%fused_computation.82 | loop fusion | bytes 1028 | tf_op jit(solution)/shard_map/dynamic_slice | solution.py:513
  21.7 2.0 %shard_map.124 = s32[1]{0:T(128)} custom-call(s32[8,16]{1,0:T(8,128)} %constant_dynamic-slice_fusion.facts_ref), custom_call_target="tpu_custom_call" | custom-call | tf_op jit(solution)/shard_map/pallas_call | solution.py:413
  24.3 83.1 %conditional.15 = ((bf16[4,128,512]{2,1,0:T(8,128)(2,1)}, bf16[16,128,512]{2,1,0:T(8,128)(2,1)}, bf16[32,576,128]{2,1,0:T(8,128)(2,1)}, bf16[32,4,128]{2,1,0:T(4,128)(2,1)})) conditional(s32[]{:T(128)} %convert_element_type.45, (s32[]{:T(128)}, s32[4]{0:T(128)}, bf16[4,576,128]{2,1,0:T(8,128)(2,1)}, bf16[4,576,256]{2,1,0:T(8,128)(2,1)S(1)}, ...), branch_computations={%region_0.15_spmd, %region_15.30_spmd} | conditional | flops 2717908992 | bytes 67062848 | solution.py:430
  25.1 81.9 %conditional.13 = ((bf16[4,128,512]{2,1,0:T(8,128)(2,1)}, bf16[16,128,512]{2,1,0:T(8,128)(2,1)}, bf16[32,576,128]{2,1,0:T(8,128)(2,1)}, bf16[32,4,128]{2,1,0:T(4,128)(2,1)})) conditional(s32[]{:T(128)} %convert_element_type.43, (s32[]{:T(128)}, s32[4]{0:T(128)}, bf16[4,576,128]{2,1,0:T(8,128)(2,1)}, bf16[4,576,256]{2,1,0:T(8,128)(2,1)S(1)}, ...), branch_computations={%region_16.22_spmd, %region_23.29_spmd} | conditional | flops 2717908992 | bytes 67062832 | solution.py:430
  25.7 81.0 %conditional.9 = ((bf16[4,128,512]{2,1,0:T(8,128)(2,1)}, bf16[16,128,512]{2,1,0:T(8,128)(2,1)}, bf16[32,576,128]{2,1,0:T(8,128)(2,1)}, bf16[32,4,128]{2,1,0:T(4,128)(2,1)})) conditional(s32[]{:T(128)} %convert_element_type.39, (s32[]{:T(128)}, s32[4]{0:T(128)}, bf16[4,576,128]{2,1,0:T(8,128)(2,1)}, bf16[4,576,256]{2,1,0:T(8,128)(2,1)S(1)}, ...), branch_computations={%region_17.18_spmd, %region_20.21_spmd} | conditional | flops 2717908992 | bytes 67062816 | solution.py:430
  26.2 80.5 %conditional.8 = (bf16[4,128,512]{2,1,0:T(8,128)(2,1)}, bf16[16,128,512]{2,1,0:T(8,128)(2,1)}, bf16[32,576,128]{2,1,0:T(8,128)(2,1)}, bf16[32,4,128]{2,1,0:T(4,128)(2,1)}) conditional(s32[]{:T(128)} %convert_element_type.38, (s32[4]{0:T(128)}, bf16[4,576,128]{2,1,0:T(8,128)(2,1)}, bf16[4,576,256]{2,1,0:T(8,128)(2,1)S(1)}, ...), branch_computations={%region_21.19_spmd, %region_22.20_spmd} | conditional | flops 2717908992 | bytes 58428380 | solution.py:430
  26.3 3.4 %dynamic-slice_bitcast_fusion.50 = (bf16[3776,128]{1,0:T(8,128)(2,1)}, bf16[3776,128]{1,0:T(8,128)(2,1)}, bf16[3776,128]{1,0:T(8,128)(2,1)}) fusion(bf16[4,4640,128]{2,1,0:T(8,128)(2,1)} %get-tuple-element.890, s32[]{:T(128)S(6)} %select_n.779, s32[]{:T(128)S(6)} %select_n.776, s32[]{:T(128)S(6)} %select_n.773), kind=kLoop, calls=%fused_computation.50 | loop fusion | bytes 5799948 | tf_op jit(solution)/shard_map/cond/branch_1_fun/cond/branch_0_fun/cond/branch_1_fun/cond/branch_0_fun/squeeze | solution.py:448
  30.5 1.5 %dynamic-slice_bitcast_fusion.53 = (bf16[2336,128]{1,0:T(8,128)(2,1)S(1)}, bf16[2336,128]{1,0:T(8,128)(2,1)S(1)}) fusion(bf16[4,4640,128]{2,1,0:T(8,128)(2,1)} %get-tuple-element.890, s32[]{:T(128)S(6)} %select_n.785, s32[]{:T(128)S(6)} %select_n.786, s32[]{:T(128)S(6)} %select_n.782), kind=kLoop, calls=%fused_computation.53 | loop fusion | bytes 2392076 | tf_op jit(solution)/shard_map/cond/branch_1_fun/cond/branch_0_fun/cond/branch_1_fun/cond/branch_0_fun/squeeze | solution.py:448
  31.9 2.7 %collective-permute-start.54 = (bf16[2336,128]{1,0:T(8,128)(2,1)S(1)}, bf16[2336,128]{1,0:T(8,128)(2,1)S(1)}, u32[]{:S(2)}, u32[]{:S(2)}) collective-permute-start(bf16[2336,128]{1,0:T(8,128)(2,1)S(1)} %get-tuple-element.1090), channel_id=1, source_target_pairs={{0,14},{2,12},{4,6},{6,4},{8,10},{10,8},{12,2},{14,0},{1,15},{3,13... | collective-permute-start | bytes 1794056 | tf_op jit(solution)/shard_map/cond/branch_1_fun/cond/branch_0_fun/cond/branch_1_fun/cond/branch_0_fun/ppermute | solution.py:449
  34.8 4.5 %branch_0_fun.39 = bf16[4,128,512]{2,1,0:T(8,128)(2,1)} custom-call(s32[4]{0:T(128)S(1)} %copy-done.63, bf16[4,576,128]{2,1,0:T(8,128)(2,1)} %get-tuple-element.882.query_ref, bf16[4,576,256]{2,1,0:T(8,128)(2,1)S(1)} %get-tuple-element.883.cache_ref, bf16[4,4,256]{2,1,0:T(4,128)(2,1)S(1)} %copy-done.35), custom_call_target="tpu_custom_call" | custom-call | flops 301989888 | bytes 2293760 | tf_op jit(solution)/shard_map/cond/branch_1_fun/cond/branch_0_fun/cond/branch_1_fun/cond/branch_0_fun/pallas_call | solution.py:58
  39.3 11.0 %branch_0_fun.40 = bf16[16,128,512]{2,1,0:T(8,128)(2,1)} custom-call(s32[16]{0:T(128)S(1)} %copy-done.49, bf16[16,576,128]{2,1,0:T(8,128)(2,1)S(1)} %copy-done.11, bf16[16,576,128]{2,1,0:T(8,128)(2,1)S(1)} %get-tuple-element.887.cache_ref, bf16[16,4,128]{2,1,0:T(4,128)(2,1)S(1)} %get-tuple-element.888.scales_ref), custom_call_target="tpu_custom_call" | custom-call | flops 603979776 | bytes 6815744 | tf_op jit(solution)/shard_map/cond/branch_1_fun/cond/branch_0_fun/cond/branch_1_fun/cond/branch_0_fun/pallas_call | solution.py:58
  50.4 37.5 %collective-permute-done.54.g4 = bf16[2336,128]{1,0:T(8,128)(2,1)S(1)} collective-permute-done((bf16[2336,128]{1,0:T(8,128)(2,1)S(1)}, bf16[2336,128]{1,0:T(8,128)(2,1)S(1)}, u32[]{:S(2)}, u32[]{:S(2)}) %collective-permute-start.54) | collective-permute-done | bytes 598048 | tf_op jit(solution)/shard_map/cond/branch_1_fun/cond/branch_0_fun/cond/branch_1_fun/cond/branch_0_fun/ppermute | solution.py:449
  87.9 11.7 %collective-permute-done.53.g3 = bf16[2336,128]{1,0:T(8,128)(2,1)S(1)} collective-permute-done((bf16[2336,128]{1,0:T(8,128)(2,1)S(1)}, bf16[2336,128]{1,0:T(8,128)(2,1)S(1)}, u32[]{:S(2)}, u32[]{:S(2)}) %collective-permute-start.53) | collective-permute-done | bytes 598048 | tf_op jit(solution)/shard_map/cond/branch_1_fun/cond/branch_0_fun/cond/branch_1_fun/cond/branch_0_fun/ppermute | solution.py:449
  99.6 0.8 copy-done.93
  100.4 6.3 %branch_0_fun.41 = (bf16[32,576,128]{2,1,0:T(8,128)(2,1)}, bf16[32,4,128]{2,1,0:T(4,128)(2,1)}) custom-call(s32[8,16]{1,0:T(8,128)S(1)} %copy-done.77, bf16[3776,128]{1,0:T(8,128)(2,1)} %collective-permute-done.50.g0, bf16[3776,128]{1,0:T(8,128)(2,1)} %collective-permute-done.51.g1, bf16[3776,128]{1,0:T(8,128)(2,1)} %collective-permute-done.52.g2, ...), custom_call_target="tpu_custom_call" | custom-call | flops 1811939328 | bytes 10485760 | tf_op jit(solution)/shard_map/cond/branch_1_fun/cond/branch_0_fun/cond/branch_1_fun/cond/branch_0_fun/pallas_call | solution.py:347
  (37 shorter events, 1.4 us)
Async XLA Ops:
  1.3 1.3 %collective-permute-start.80 = (s32[16]{0:T(128)S(1)}, s32[16]{0:T(128)S(1)}, u32[]{:S(2)}, u32[]{:S(2)}) collective-permute-start(s32[16]{0:T(128)S(1)} %multiply_add_fusion), channel_id=1, source_target_pairs={{0,2},{2,0},{1,3},{3,1},{4,6},{6,4},{5,7},{7,5},{8,10},{10,8},{9,1... | collective-permute-start | bytes 200 | tf_op jit(solution)/shard_map/ppermute | solution.py:509
  2.6 6.9 %copy-start.86 = (s32[16]{0:T(128)}, s32[16]{0:T(128)S(1)}, u32[]{:S(2)}) copy-start(s32[16]{0:T(128)S(1)} %collective-permute-done.80.after_ref) | copy-start | bytes 196
  2.6 14.0 %copy-start.83 = (s32[2,16]{1,0:T(2,128)}, s32[2,16]{1,0:T(2,128)S(1)}, u32[]{:S(2)}) copy-start(s32[2,16]{1,0:T(2,128)S(1)} %add_select_fusion) | copy-start | bytes 388
  2.6 14.0 %collective-permute-start.83 = (s32[2,16]{1,0:T(2,128)S(1)}, s32[2,16]{1,0:T(2,128)S(1)}, u32[]{:S(2)}, u32[]{:S(2)}) collective-permute-start(s32[2,16]{1,0:T(2,128)S(1)} %add_select_fusion), channel_id=1, source_target_pairs={{0,4},{4,8},{8,12},{12,0},{1,5},{5,9},{9,13},{13,1},{2,6},{6,10},{... | collective-permute-start | bytes 392 | tf_op jit(solution)/shard_map/ppermute | solution.py:511
  5.5 11.1 %collective-permute-start.82 = (s32[2,16]{1,0:T(2,128)S(1)}, s32[2,16]{1,0:T(2,128)S(1)}, u32[]{:S(2)}, u32[]{:S(2)}) collective-permute-start(s32[2,16]{1,0:T(2,128)S(1)} %add_select_fusion), channel_id=1, source_target_pairs={{0,8},{4,12},{8,0},{12,4},{1,9},{5,13},{9,1},{13,5},{2,10},{6,14},... | collective-permute-start | bytes 392 | tf_op jit(solution)/shard_map/ppermute | solution.py:511
  8.1 9.6 %collective-permute-start.81 = (s32[2,16]{1,0:T(2,128)S(1)}, s32[2,16]{1,0:T(2,128)}, u32[]{:S(2)}, u32[]{:S(2)}) collective-permute-start(s32[2,16]{1,0:T(2,128)S(1)} %add_select_fusion), channel_id=1, source_target_pairs={{0,12},{4,0},{8,4},{12,8},{1,13},{5,1},{9,5},{13,9},{2,14},{6,2},{... | collective-permute-start | bytes 392 | tf_op jit(solution)/shard_map/ppermute | solution.py:511
  9.5 14.8 %copy-start = (bf16[16,128,576]{1,2,0:T(8,128)(2,1)S(1)}, bf16[16,128,576]{1,2,0:T(8,128)(2,1)}, u32[]{:S(2)}) copy-start(bf16[16,128,576]{1,2,0:T(8,128)(2,1)} %param.43) | copy-start | bytes 7077892
  9.5 14.8 %copy-start.17 = (bf16[4,256,576]{1,2,0:T(8,128)(2,1)S(1)}, bf16[4,256,576]{1,2,0:T(8,128)(2,1)}, u32[]{:S(2)}) copy-start(bf16[4,256,576]{1,2,0:T(8,128)(2,1)} %param.39) | copy-start | bytes 3538948
  9.5 14.8 %copy-start.26 = (bf16[16,4,128]{2,1,0:T(4,128)(2,1)S(1)}, bf16[16,4,128]{2,1,0:T(4,128)(2,1)}, u32[]{:S(2)}) copy-start(bf16[16,4,128]{2,1,0:T(4,128)(2,1)} %scales_ref.1) | copy-start | bytes 49156
  16.6 0.6 copy-start.84
  17.2 0.6 copy-start.85
  29.7 69.9 %collective-permute-start.52 = (bf16[3776,128]{1,0:T(8,128)(2,1)}, bf16[3776,128]{1,0:T(8,128)(2,1)}, u32[]{:S(2)}, u32[]{:S(2)}) collective-permute-start(bf16[3776,128]{1,0:T(8,128)(2,1)} %get-tuple-element.1092), channel_id=1, source_target_pairs={{0,2},{2,0},{4,14},{6,12},{8,10},{10,8},{12,6},{14,4},{1,3},{3,1},... | collective-permute-start | bytes 2899976 | tf_op jit(solution)/shard_map/cond/branch_1_fun/cond/branch_0_fun/cond/branch_1_fun/cond/branch_0_fun/ppermute | solution.py:449
  29.7 69.9 %collective-permute-start.51 = (bf16[3776,128]{1,0:T(8,128)(2,1)}, bf16[3776,128]{1,0:T(8,128)(2,1)}, u32[]{:S(2)}, u32[]{:S(2)}) collective-permute-start(bf16[3776,128]{1,0:T(8,128)(2,1)} %get-tuple-element.1093), channel_id=1, source_target_pairs={{0,2},{2,0},{4,10},{6,8},{8,6},{10,4},{12,14},{14,12},{1,3},{3,1},... | collective-permute-start | bytes 2899976 | tf_op jit(solution)/shard_map/cond/branch_1_fun/cond/branch_0_fun/cond/branch_1_fun/cond/branch_0_fun/ppermute | solution.py:449
  30.2 69.4 %collective-permute-start.50 = (bf16[3776,128]{1,0:T(8,128)(2,1)}, bf16[3776,128]{1,0:T(8,128)(2,1)}, u32[]{:S(2)}, u32[]{:S(2)}) collective-permute-start(bf16[3776,128]{1,0:T(8,128)(2,1)} %get-tuple-element.1094), channel_id=1, source_target_pairs={{0,6},{2,4},{4,2},{6,0},{8,14},{10,12},{12,10},{14,8},{1,7},{3,5},... | collective-permute-start | bytes 2899976 | tf_op jit(solution)/shard_map/cond/branch_1_fun/cond/branch_0_fun/cond/branch_1_fun/cond/branch_0_fun/ppermute | solution.py:449
  30.4 4.3 %copy-start.35 = (bf16[4,4,256]{2,1,0:T(4,128)(2,1)S(1)}, bf16[4,4,256]{2,1,0:T(4,128)(2,1)}, u32[]{:S(2)}) copy-start(bf16[4,4,256]{2,1,0:T(4,128)(2,1)} %get-tuple-element.884.scales_ref) | copy-start | bytes 24580 | tf_op jit(solution)/shard_map/cond/branch_1_fun/cond/branch_0_fun/cond/branch_1_fun/cond
  30.4 4.3 %copy-start.63 = (s32[4]{0:T(128)S(1)}, s32[4]{0:T(128)}, u32[]{:S(2)}) copy-start(s32[4]{0:T(128)} %get-tuple-element.881.lengths_ref) | copy-start | bytes 52 | tf_op jit(solution)/shard_map/cond/branch_1_fun/cond/branch_0_fun/cond/branch_1_fun/cond
  30.4 8.9 %copy-start.11 = (bf16[16,576,128]{2,1,0:T(8,128)(2,1)S(1)}, bf16[16,576,128]{2,1,0:T(8,128)(2,1)}, u32[]{:S(2)}) copy-start(bf16[16,576,128]{2,1,0:T(8,128)(2,1)} %get-tuple-element.886.query_ref) | copy-start | bytes 7077892 | tf_op jit(solution)/shard_map/cond/branch_1_fun/cond/branch_0_fun/cond/branch_1_fun/cond
  30.4 8.9 %copy-start.49 = (s32[16]{0:T(128)S(1)}, s32[16]{0:T(128)}, u32[]{:S(2)}) copy-start(s32[16]{0:T(128)} %get-tuple-element.885.lengths_ref) | copy-start | bytes 196 | tf_op jit(solution)/shard_map/cond/branch_1_fun/cond/branch_0_fun/cond/branch_1_fun/cond
  31.9 55.9 %collective-permute-start.54 = (bf16[2336,128]{1,0:T(8,128)(2,1)S(1)}, bf16[2336,128]{1,0:T(8,128)(2,1)S(1)}, u32[]{:S(2)}, u32[]{:S(2)}) collective-permute-start(bf16[2336,128]{1,0:T(8,128)(2,1)S(1)} %get-tuple-element.1090), channel_id=1, source_target_pairs={{0,14},{2,12},{4,6},{6,4},{8,10},{10,8},{12,2},{14,0},{1,15},{3,13... | collective-permute-start | bytes 1794056 | tf_op jit(solution)/shard_map/cond/branch_1_fun/cond/branch_0_fun/cond/branch_1_fun/cond/branch_0_fun/ppermute | solution.py:449
  34.6 64.9 %collective-permute-start.53 = (bf16[2336,128]{1,0:T(8,128)(2,1)S(1)}, bf16[2336,128]{1,0:T(8,128)(2,1)S(1)}, u32[]{:S(2)}, u32[]{:S(2)}) collective-permute-start(bf16[2336,128]{1,0:T(8,128)(2,1)S(1)} %get-tuple-element.1091), channel_id=1, source_target_pairs={{0,10},{2,8},{4,6},{6,4},{8,2},{10,0},{12,14},{14,12},{1,11},{3,9}... | collective-permute-start | bytes 1794056 | tf_op jit(solution)/shard_map/cond/branch_1_fun/cond/branch_0_fun/cond/branch_1_fun/cond/branch_0_fun/ppermute | solution.py:449
  39.3 61.1 %copy-start.77 = (s32[8,16]{1,0:T(8,128)S(1)}, s32[8,16]{1,0:T(8,128)}, u32[]{:S(2)}) copy-start(s32[8,16]{1,0:T(8,128)} %get-tuple-element.889.facts_ref) | copy-start | bytes 1540 | tf_op jit(solution)/shard_map/cond/branch_1_fun/cond/branch_0_fun/cond/branch_1_fun/cond
  87.9 11.8 %copy-start.89 = (bf16[2336,128]{1,0:T(8,128)(2,1)}, bf16[2336,128]{1,0:T(8,128)(2,1)S(1)}, u32[]{:S(2)}) copy-start(bf16[2336,128]{1,0:T(8,128)(2,1)S(1)} %collective-permute-done.54.g4) | copy-start | bytes 1794052 | tf_op jit(solution)/shard_map/cond/branch_1_fun/cond/branch_0_fun/cond/branch_1_fun/cond
  99.6 0.8 copy-start.93
